TPU v7x, 32 devices: a whole 2x2x4 slice. The times are simulated.
32 devices in a mesh: dp: 4 (over y, x), tensor: 8 (over z, core).
Axes of the slice: x: 2, y: 2, z: 4, core: 2. Of those that a mesh axis runs over, the one named last changes fastest.
Arguments:
- acts: bfloat16 [4096, 28672], P('dp', 'tensor'), may hold values from -6 to 6
- out_grads: bfloat16 [4096, 8192], P('dp', 'tensor'), may hold values from -4 to 4
- proj_in: bfloat16 [28672, 64], P('tensor'), may hold values from -0.03125 to 0.03125
- proj_out: bfloat16 [8192, 64], P('tensor'), may hold values from -0.0625 to 0.0625
- doc_lengths: int32 [4, 4], P('dp'), may hold values from 1 to 512, 1024 in all within a row
- owner_map: int32 [4, 4], P('dp'), may hold values from 0 to 3, each once within a row
Outputs:
- doc_grads: float32 [16, 4096], P('dp', 'tensor')
Inputs may be any that keep to these rules, and one draw needn't show every extreme that they name: `doc_lengths`: each row sums to 1024 and its largest entry is 512. `owner_map`: each row is a permutation of the owners.
All inputs are finite; a program needn't handle non-finite values.
Results may differ from a plain program's by a relative error of at most 0.0003.
Values may be sent and summed in bfloat16 or wider, within the bound.
No kernel may reach another device: no remote copies, remote signals or barrier semaphores. Data moves between devices by JAX's collectives and lax.ppermute only.
A program may use at most 64 MiB of HBM per device.

v0:
```python
import jax
import jax.numpy as jnp
from jax import lax
from jax.sharding import PartitionSpec as P


def on_device(acts, out_grads, proj_in, proj_out, doc_lengths, owner_map):
    owners = lax.axis_size("dp")
    length = acts.shape[0]
    capacity = 2 * length // owners
    proj_rank = proj_in.shape[1]
    doc_len = doc_lengths[0]
    doc_owner = owner_map[0]
    doc_start = jnp.cumsum(doc_len) - doc_len
    matches = (doc_owner[None, :] == jnp.arange(owners, dtype=jnp.int32)[:, None]).astype(jnp.int32)
    first_row = jnp.sum(matches * doc_start[None, :], axis=1)
    live_rows = jnp.sum(matches * doc_len[None, :], axis=1)
    is_live = jnp.arange(capacity, dtype=jnp.int32)[None, :] < live_rows[:, None]
    in_side = jnp.dot(acts, proj_in, preferred_element_type=jnp.float32)
    out_side = jnp.dot(out_grads, proj_out, preferred_element_type=jnp.float32)
    source = jnp.concatenate([in_side, out_side], -1)
    padded = jnp.concatenate([source, jnp.zeros((capacity, source.shape[1]), source.dtype)], 0)
    sliced = jax.vmap(lambda offset: lax.dynamic_slice_in_dim(padded, offset, capacity, 0))(
        first_row
    )
    partial_value = jnp.where(is_live[:, :, None], sliced, jnp.zeros((), source.dtype))
    reduced = lax.all_to_all(
        lax.psum_scatter(partial_value, "tensor", scatter_dimension=1, tiled=True),
        "dp",
        split_axis=0,
        concat_axis=0,
        tiled=True,
    )
    in_side = reduced[:, :, :proj_rank]
    out_side = reduced[:, :, proj_rank:]
    grads = jnp.einsum("sci,scj->sij", out_side, in_side, precision=lax.Precision.HIGHEST)
    grads = grads.reshape(owners, proj_rank * proj_rank)
    return lax.psum_scatter(grads, "tensor", scatter_dimension=1, tiled=True)


def solution(mesh):
    in_specs = (
        P("dp", "tensor"),
        P("dp", "tensor"),
        P("tensor", None),
        P("tensor", None),
        P("dp", None),
        P("dp", None),
    )
    out_specs = P("dp", "tensor")
    return jax.shard_map(
        on_device, mesh=mesh, in_specs=in_specs, out_specs=out_specs, check_vma=False
    )
```

profile of v0, /device:TPU:0, one launch (start us, length us, event | category | flops | bytes accessed | tf_op | source)
XLA Modules:
  0.0 115.0 jit_solution(11624899259497863165)
XLA Ops:
  6.5 1.0 reduce-window_clone.1
  7.5 0.7 subtract_bitcast_fusion
  8.2 0.8 select_reduce_fusion.1
  9.0 5.4 %fusion.3 = f32[1024,64]{0,1:T(8,128)S(1)} fusion(bf16[1024,3584]{1,0:T(8,128)(2,1)} %param.6, bf16[3584,64]{0,1:T(8,128)(2,1)} %param.8), kind=kOutput, calls=%fused_computation.15 | convolution fusion | flops 469762048 | bytes 8060928 | tf_op jit(solution)/shard_map/dot_general | solution.py:19
  14.5 0.8 fusion.4
  15.3 0.1 select_maximum_fusion
  15.3 9.5 %while.2 = (s32[]{:T(128)}, f32[1536,128]{0,1:T(8,128)S(1)}, s32[4,2]{0,1:T(2,128)S(1)}, f32[4,512,128]{2,1,0:T(8,128)}) while((s32[]{:T(128)}, f32[1536,128]{0,1:T(8,128)S(1)}, s32[4,2]{0,1:T(2,128)S(1)}, f32[4,512,128]{2,1,0:T(8,128)}) %tuple.23), condition=%wide.while_cond.clone, body=%wide.while_body.sunk.clone | while | flops 2 | bytes 1573461 | solution.py:23
  15.4 0.1 constant_dynamic-slice_fusion.6
  15.4 0.6 slice.27
  16.0 0.8 constant_dynamic-slice_fusion.7
  16.9 0.1 copy.20
  17.0 0.7 bitcast_dynamic-update-slice_fusion.3
  17.8 0.6 slice.27
  18.4 0.8 constant_dynamic-slice_fusion.7
  19.2 0.1 copy.20
  19.4 0.7 bitcast_dynamic-update-slice_fusion.3
  20.2 0.6 slice.27
  20.8 0.8 constant_dynamic-slice_fusion.7
  21.6 0.1 copy.20
  21.7 0.7 bitcast_dynamic-update-slice_fusion.3
  22.5 0.6 slice.27
  23.1 0.8 constant_dynamic-slice_fusion.7
  23.9 0.1 copy.20
  24.1 0.7 bitcast_dynamic-update-slice_fusion.3
  24.8 0.1 iota_compare_fusion.1
  24.9 2.6 %broadcast_select_fusion = f32[4,512,128]{2,1,0:T(8,128)} fusion(f32[4,512,128]{2,1,0:T(8,128)} %get-tuple-element.12, pred[4,512]{1,0:T(4,128)(4,1)S(1)} %iota_compare_fusion.1), kind=kLoop, calls=%fused_computation.5 | loop fusion | flops 262144 | bytes 2099200 | tf_op jit(solution)/shard_map/jit(_where)/select_n | solution.py:26
  27.5 35.1 %reduce-scatter.5.cloned.1.call-done = f32[4,64,128]{2,1,0:T(8,128)} async-done(((f32[4,512,128]{2,1,0:T(8,128)}), f32[4,64,128]{2,1,0:T(8,128)}) %reduce-scatter.5.cloned.1.call-update) | async-done | bytes 131088 | tf_op jit(solution)/shard_map/reduce_scatter | solution.py:28
  62.6 8.7 %all_to_all.5 = f32[4,64,128]{2,1,0:T(8,128)S(1)} all-to-all(f32[4,64,128]{2,1,0:T(8,128)} %reduce-scatter.5.cloned.1.call-done), channel_id=1, replica_groups=mesh['dp'=4,'tensor'=8] {'dp'}, dimensions={0} | all-to-all | bytes 262144 | tf_op jit(solution)/shard_map/all_to_all | solution.py:27
  71.3 0.5 fusion
  71.8 2.1 %copy.16 = f32[4,64,64]{0,2,1:T(8,128)} copy(f32[4,64,64]{2,1,0:T(8,128)S(1)} %fusion) | data formatting | bytes 131072
  73.9 32.6 %reduce-scatter.7.cloned.1.call-done = f32[512,4]{1,0:T(8,128)} async-done(((f32[4096,4]{1,0:T(8,128)}), f32[512,4]{1,0:T(8,128)}) %reduce-scatter.7.cloned.1.call-update) | async-done | bytes 8208
  106.5 1.7 %copy.15 = f32[4,512]{1,0:T(4,128)} copy(f32[4,512]{0,1:T(8,128)} %bitcast.24) | data formatting | bytes 16384
  (14 shorter events, 0.3 us)
Async XLA Ops:
  6.5 7.9 %copy-start = (bf16[1024,1024]{1,0:T(8,128)(2,1)S(1)}, bf16[1024,1024]{1,0:T(8,128)(2,1)}, u32[]{:S(2)}) copy-start(bf16[1024,1024]{1,0:T(8,128)(2,1)} %param.7) | copy-start | bytes 6291460
  6.5 56.1 %reduce-scatter.5.cloned.1.call-start = ((), (), s32[]{:S(2)}) async-start(), calls=%async_computation.3 | async-start | bytes 1179648 | tf_op jit(solution)/shard_map/reduce_scatter | solution.py:28
  9.0 5.5 %copy-start.1 = (bf16[1024,64]{0,1:T(8,128)(2,1)S(1)}, bf16[1024,64]{0,1:T(8,128)(2,1)}, u32[]{:S(2)}) copy-start(bf16[1024,64]{0,1:T(8,128)(2,1)} %param.9) | copy-start | bytes 393220
  27.5 79.0 %reduce-scatter.7.cloned.1.call-start = ((), (), s32[]{:S(2)}) async-start(), calls=%async_computation.4 | async-start | bytes 2359296
Sparse Core Ops, SparseCore 0:
  27.6 34.9 reduce-scatter.4
  74.0 32.4 reduce-scatter.6
where the time goes:
time: 115 us
  waiting for transfers between devices  67.7 us (59%)
  between operations  13.5 us (12%)
  local copies, waits for them, and re-layouts  13.1 us (11%)
  blocking collectives  8.7 us (8%)
  matrix products  6.67 us (6%)
  other arithmetic  5.16 us (4%)
    reduce_scatter x1, waiting for transfers between devices, on_device(): lax.psum_scatter(partial_value, 'tensor', scatter_dimension=1, tiled=True)  35.1 us
    unnamed x3, waiting for transfers between devices  32.6 us
    gather x20, local copies, waits for them, and re-layouts  9.39 us
    all_to_all x1, blocking collectives, on_device(): lax.all_to_all(lax.psum_scatter(partial_value, 'tensor', scatter_dimensio...  8.7 us
    dot_general x1, matrix products, on_device(): in_side = jnp.dot(acts, proj_in, preferred_element_type=jnp.float32)  5.45 us
    unnamed x6, local copies, waits for them, and re-layouts  3.74 us
    select_n x1, other arithmetic, on_device(): jnp.where(is_live[:, :, None], sliced, jnp.zeros((), source.dtype))  2.55 us
  transfers between devices with their start and end apart: 2, of which 2 were waited for; matrix products, arithmetic and copies ran while one was open for 0% of the time, Pallas kernels for 0%

commit v1 on v0

v1 whole, which is shorter than its diff:
```python
import functools
import math
import jax
import jax.numpy as jnp
from jax import lax
from jax.experimental import pallas as pl
from jax.experimental.pallas import tpu as pltpu
from jax.sharding import PartitionSpec as P

NT = (((1,), (1,)), ((), ()))


def project(place, acts_hbm, grads_hbm, in_hbm, out_hbm, kept, sent, held, weights, w_sems, sems):
    rank = in_hbm.shape[0]
    chunks, length, depth = held.shape
    hidden, width = acts_hbm.shape[1], grads_hbm.shape[1]
    half = length // 2
    rows = half // 2
    ahead = min(4, chunks)

    def copy(i):
        if i * depth < width:
            source = grads_hbm.at[:, pl.ds(i * depth, depth)]
        else:
            source = acts_hbm.at[:, pl.ds(i * depth - width, depth)]
        return pltpu.make_async_copy(source, held.at[i], sems.at[i])

    loads = (
        pltpu.make_async_copy(
            out_hbm, weights.at[pl.ds(rank, rank), pl.ds(0, width)], w_sems.at[0]
        ),
        pltpu.make_async_copy(
            in_hbm, weights.at[pl.ds(0, rank), pl.ds(width, hidden)], w_sems.at[1]
        ),
    )
    for load in loads:
        load.start()
    for i in range(ahead):
        copy(i).start()
    weights[pl.ds(0, rank), pl.ds(0, width)] = jnp.zeros((rank, width), weights.dtype)
    weights[pl.ds(rank, rank), pl.ds(width, hidden)] = jnp.zeros((rank, hidden), weights.dtype)
    for load in loads:
        load.wait()
    core = place[0]
    for i in range(chunks):
        copy(i).wait()
        if i + ahead < chunks:
            copy(i + ahead).start()
        block = weights[:, i * depth : (i + 1) * depth]
        for out, base in ((sent, (1 - core) * half), (kept, core * half)):
            for at in range(0, half, rows):
                part = held[i, pl.ds(pl.multiple_of(base + at, rows), rows), :]
                term = lax.dot_general(part, block, NT, preferred_element_type=jnp.float32)
                if i:
                    out[pl.ds(at, rows), :] += term
                else:
                    out[pl.ds(at, rows), :] = term


def outer(doc_len, doc_owner, place, parts, out, turned, picked):
    slots, tokens, lanes = parts.shape
    docs = doc_len.shape[1]
    owners = out.shape[0]
    rank = lanes // 2
    half = rank // 2
    rows = parts[0]
    for i in range(1, slots):
        rows = rows + parts[i]
    turned[...] = rows.T
    lane = lax.broadcasted_iota(jnp.int32, rows.shape, 1)
    left = jnp.where(lane < rank, rows, 0.0)
    right = jnp.where(lane < rank, 0.0, pltpu.roll(rows, rank, 1))
    even = turned[pl.ds(rank, half, stride=2), :]
    odd = turned[pl.ds(rank + 1, half, stride=2), :]
    at = place[1] + lax.broadcasted_iota(jnp.int32, even.shape, 1)
    starts = []
    start = jnp.int32(0)
    for k in range(docs):
        starts.append(start)
        start = start + doc_len[0, k]
    for o in range(owners):
        first, last = jnp.int32(0), jnp.int32(0)
        for k in range(docs):
            mine = doc_owner[0, k] == o
            first = jnp.where(mine, starts[k], first)
            last = jnp.where(mine, starts[k] + doc_len[0, k], last)
        live = (at >= first) & (at < last)
        picked[0, pl.ds(o * half, half), :] = jnp.where(live, even, 0.0)
        picked[1, pl.ds(o * half, half), :] = jnp.where(live, odd, 0.0)
    dot = functools.partial(
        jnp.dot, precision=lax.Precision.HIGHEST, preferred_element_type=jnp.float32
    )
    grads = dot(picked[0], left) + dot(picked[1], right)
    out[...] = grads.reshape(out.shape)


def collect(parts, out):
    seqs, width = out.shape
    lanes = parts.shape[1]
    blocks = width // lanes
    terms = parts.shape[0] // (seqs * blocks)
    for s in range(seqs):
        for c in range(blocks):
            block = parts[pl.ds(s * terms * blocks + c, terms, stride=blocks), :]
            out[pl.ds(s, 1), pl.ds(c * lanes, lanes)] = jnp.sum(block, axis=0, keepdims=True)


def on_device(acts, out_grads, proj_in, proj_out, doc_lengths, owner_map):
    owners = lax.axis_size("dp")
    split = lax.axis_size("tensor")
    length, hidden = acts.shape
    width = out_grads.shape[1]
    rank = proj_in.shape[1]
    lanes = 2 * rank
    depth = math.gcd(512, math.gcd(hidden, width))
    pairs = split // 2
    tokens = length // split
    vmem = pl.BlockSpec(memory_space=pltpu.VMEM)
    smem = pl.BlockSpec(memory_space=pltpu.SMEM)
    hbm = pl.BlockSpec(memory_space=pl.ANY)

    at = lax.axis_index("tensor")
    core, pair = at % 2, at // 2
    place = jnp.stack([core, core * (length // 2) + pair * tokens]).astype(jnp.int32)
    half = pltpu.VMEM((length // 2, lanes), jnp.float32)
    kept, sent = pl.pallas_call(
        project,
        out_shape=(half, half),
        in_specs=[smem] + [hbm] * 4,
        out_specs=(vmem, vmem),
        scratch_shapes=[
            pltpu.VMEM(((hidden + width) // depth, length, depth), acts.dtype),
            pltpu.VMEM((lanes, hidden + width), proj_in.dtype),
            pltpu.SemaphoreType.DMA((2,)),
            pltpu.SemaphoreType.DMA(((hidden + width) // depth,)),
        ],
        compiler_params=pltpu.CompilerParams(vmem_limit_bytes=56 << 20),
    )(place, acts, out_grads, proj_in.T, proj_out.T)
    got = lax.ppermute(sent, "tensor", [(i, i ^ 1) for i in range(split)])
    halves = (kept + got).reshape(pairs, tokens, lanes)
    parts = jnp.stack(
        [lax.dynamic_index_in_dim(halves, pair, 0, keepdims=False)]
        + [
            lax.ppermute(
                lax.dynamic_index_in_dim(halves, pair ^ m, 0, keepdims=False),
                "tensor",
                [(i, i ^ (2 * m)) for i in range(split)],
            )
            for m in range(1, pairs)
        ]
    )
    grads = pl.pallas_call(
        outer,
        out_shape=pltpu.VMEM((owners, rank // 2, lanes), jnp.float32),
        in_specs=[smem, smem, smem, vmem],
        out_specs=vmem,
        scratch_shapes=[
            pltpu.VMEM((lanes, tokens), jnp.float32),
            pltpu.VMEM((2, owners * rank // 2, tokens), jnp.float32),
        ],
        compiler_params=pltpu.CompilerParams(vmem_limit_bytes=8 << 20),
    )(doc_lengths, owner_map, place, parts)
    got = lax.all_to_all(
        grads.reshape(owners * rank // 2, lanes), ("dp", "tensor"), 0, 0, tiled=True
    )
    return pl.pallas_call(
        collect,
        out_shape=jax.ShapeDtypeStruct((owners, rank * rank // split), jnp.float32),
        in_specs=[vmem],
        out_specs=vmem,
        compiler_params=pltpu.CompilerParams(vmem_limit_bytes=8 << 20),
    )(got)


def solution(mesh):
    in_specs = (
        P("dp", "tensor"),
        P("dp", "tensor"),
        P("tensor", None),
        P("tensor", None),
        P("dp", None),
        P("dp", None),
    )
    out_specs = P("dp", "tensor")
    return jax.shard_map(
        on_device, mesh=mesh, in_specs=in_specs, out_specs=out_specs, check_vma=False
    )
```

time: 115 us -> 32.8 us (0.29)
  waiting for transfers between devices: 67.7 us -> 6.4 us
  between operations: 13.5 us -> 0.06 us
  local copies, waits for them, and re-layouts: 13.1 us -> 0.04 us
  Pallas kernels: 0 us -> 7.36 us
  matrix products: 6.67 us -> 0 us
  starting transfers between devices: 0.04 us -> 6.19 us
  other arithmetic: 5.16 us -> 0.68 us
  blocking collectives: 8.7 us -> 11.9 us
    reduce_scatter x1 -> x0, waiting for transfers between devices: 35.1 us -> none  [on_device(): lax.psum_scatter(partial_value, 'tensor', scatter_dimension=1, tiled=True)]
    unnamed x3 -> x0, waiting for transfers between devices: 32.6 us -> none
    gather x20 -> x0, local copies, waits for them, and re-layouts: 9.39 us -> none
    pallas_call x0 -> x3, Pallas kernels: none -> 7.36 us  [the longest x1 5.83 us: on_device(): pl.pallas_call(project, out_shape=(half, half), in_specs=[smem] + [hbm] *...]
    dot_general x3 -> x0, matrix products: 6.67 us -> none  [the longest x1 5.45 us: on_device(): in_side = jnp.dot(acts, proj_in, preferred_element_type=jnp.float32)]
    ppermute x0 -> x4, waiting for transfers between devices: none -> 6.4 us  [the longest x3 5.24 us: on_device(): lax.ppermute(lax.dynamic_index_in_dim(halves, pair ^ m, 0, keepdims=False...]
    ppermute x0 -> x4, starting transfers between devices: none -> 6.19 us  [the longest x3 5.67 us: on_device(): lax.ppermute(lax.dynamic_index_in_dim(halves, pair ^ m, 0, keepdims=False...]
    unnamed x6, local copies, waits for them, and re-layouts: 3.74 us -> 0.01 us
  transfers between devices with their start and end apart: 2 -> 4, of which waited for: 2 -> 3; matrix products, arithmetic and copies ran while one was open for 0% -> 0% of each run, Pallas kernels for 0% -> 0%
where the time goes in v1:
time: 32.8 us; the launch traced here: 32.7 us
  blocking collectives  11.9 us (36%)
  Pallas kernels  7.36 us (22%)
  waiting for transfers between devices  6.4 us (20%)
  starting transfers between devices  6.19 us (19%)
  other arithmetic  0.68 us (2%)
    all_to_all x1, blocking collectives, on_device(): lax.all_to_all(grads.reshape(owners * rank // 2, lanes), ('dp', 'tensor')...  11.9 us
    pallas_call x1, Pallas kernels, on_device(): pl.pallas_call(project, out_shape=(half, half), in_specs=[smem] + [hbm] *...  5.83 us
    ppermute x3, starting transfers between devices, on_device(): lax.ppermute(lax.dynamic_index_in_dim(halves, pair ^ m, 0, keepdims=False...  5.67 us
    ppermute x3, waiting for transfers between devices, on_device(): lax.ppermute(lax.dynamic_index_in_dim(halves, pair ^ m, 0, keepdims=False...  5.24 us
    ppermute x1, waiting for transfers between devices, on_device(): got = lax.ppermute(sent, 'tensor', [(i, i ^ 1) for i in range(split)])  1.16 us
    pallas_call x1, Pallas kernels, on_device(): pl.pallas_call(outer, out_shape=pltpu.VMEM((owners, rank // 2, lanes), jn...  0.92 us
  transfers between devices with their start and end apart: 4, of which 3 were waited for; matrix products, arithmetic and copies ran while one was open for 0% of the time, Pallas kernels for 0%

profile of v1, /device:TPU:0, one launch (start us, length us, event | category | flops | bytes accessed | tf_op | source)
XLA Modules:
  0.0 32.7 jit_solution(15845873877344554604)
XLA Ops:
  0.0 0.0 copy-start.1
  0.0 0.0 copy-start.2
  0.0 0.6 %pad_add_fusion.place = s32[2]{0:T(128)} fusion(s32[1]{0:T(128)} %bitcast.1, s32[1]{0:T(128)} %bitcast), kind=kLoop, calls=%fused_computation.5 | loop fusion | flops 2 | bytes 16 | tf_op jit(solution)/shard_map/stack | solution.py:124
  0.6 0.0 copy-start
  0.6 5.8 %shard_map.64 = (f32[512,128]{1,0:T(8,128)S(1)}, f32[512,128]{1,0:T(8,128)S(1)}) custom-call(s32[2]{0:T(128)} %pad_add_fusion.place, bf16[1024,3584]{1,0:T(8,128)(2,1)} %acts_hbm.1, bf16[1024,1024]{1,0:T(8,128)(2,1)} %grads_hbm.1, bf16[64,3584]{1,0:T(8,128)(2,1)} %bitcast.19, bf16[64,1024]{1,0:T(8,128)(2,1)} %bitcast.20), custom_call_target="tpu_custom_call" | custom-call | tf_op jit(solution)/shard_map/pallas_call | solution.py:126
  6.5 0.5 %collective-permute-start = (f32[512,128]{1,0:T(8,128)S(1)}, f32[512,128]{1,0:T(8,128)S(1)}, u32[]{:S(2)}, u32[]{:S(2)}) collective-permute-start(f32[512,128]{1,0:T(8,128)S(1)} %get-tuple-element.8), channel_id=1, source_target_pairs={{0,1},{1,0},{2,3},{3,2},{4,5},{5,4},{6,7},{7,6},{8,9},{9,8},{10,11... | collective-permute-start | bytes 786440 | tf_op jit(solution)/shard_map/ppermute | solution.py:139
  7.0 1.2 %collective-permute-done = f32[512,128]{1,0:T(8,128)S(1)} collective-permute-done((f32[512,128]{1,0:T(8,128)S(1)}, f32[512,128]{1,0:T(8,128)S(1)}, u32[]{:S(2)}, u32[]{:S(2)}) %collective-permute-start) | collective-permute-done | bytes 262176 | tf_op jit(solution)/shard_map/ppermute | solution.py:139
  8.2 5.0 %collective-permute-start.3 = (f32[128,128]{1,0:T(8,128)S(1)}, f32[128,128]{1,0:T(8,128)S(1)}, u32[]{:S(2)}, u32[]{:S(2)}) collective-permute-start(f32[128,128]{1,0:T(8,128)S(1)} %get-tuple-element.10), channel_id=1, source_target_pairs={{0,6},{1,7},{2,4},{3,5},{4,2},{5,3},{6,0},{7,1},{8,14},{9,15},{10,... | collective-permute-start | bytes 196616 | tf_op jit(solution)/shard_map/ppermute | solution.py:144
  13.3 0.0 collective-permute-start.2
  13.3 0.6 %collective-permute-start.1 = (f32[128,128]{1,0:T(8,128)S(1)}, f32[128,128]{1,0:T(8,128)S(1)}, u32[]{:S(2)}, u32[]{:S(2)}) collective-permute-start(f32[128,128]{1,0:T(8,128)S(1)} %get-tuple-element.12), channel_id=1, source_target_pairs={{0,2},{1,3},{2,0},{3,1},{4,6},{5,7},{6,4},{7,5},{8,10},{9,11},{10,... | collective-permute-start | bytes 196616 | tf_op jit(solution)/shard_map/ppermute | solution.py:144
  13.9 2.0 %collective-permute-done.3 = f32[128,128]{1,0:T(8,128)S(1)} collective-permute-done((f32[128,128]{1,0:T(8,128)S(1)}, f32[128,128]{1,0:T(8,128)S(1)}, u32[]{:S(2)}, u32[]{:S(2)}) %collective-permute-start.3) | collective-permute-done | bytes 65568 | tf_op jit(solution)/shard_map/ppermute | solution.py:144
  15.9 3.3 %collective-permute-done.2 = f32[128,128]{1,0:T(8,128)S(1)} collective-permute-done((f32[128,128]{1,0:T(8,128)S(1)}, f32[128,128]{1,0:T(8,128)S(1)}, u32[]{:S(2)}, u32[]{:S(2)}) %collective-permute-start.2) | collective-permute-done | bytes 65568 | tf_op jit(solution)/shard_map/ppermute | solution.py:144
  19.1 0.0 collective-permute-done.1
  19.2 0.0 copy-done.1
  19.2 0.0 copy-done.2
  19.2 0.0 copy-done
  19.2 0.9 %shard_map.65 = f32[4,32,128]{2,1,0:T(8,128)S(1)} custom-call(s32[1,4]{1,0:T(1,128)S(1)} %copy-done.1, s32[1,4]{1,0:T(1,128)S(1)} %copy-done.2, s32[2]{0:T(128)S(1)} %copy-done, f32[4,128,128]{2,1,0:T(8,128)S(1)} %pad_maximum_fusion.parts), custom_call_target="tpu_custom_call" | custom-call | tf_op jit(solution)/shard_map/pallas_call | solution.py:152
  20.1 11.9 %all_to_all.11 = f32[32,4,128]{2,1,0:T(4,128)S(1)} all-to-all(f32[32,4,128]{2,1,0:T(4,128)S(1)} %bitcast.16), channel_id=1, replica_groups=mesh['dp'=4,'tensor'=8] {'dp','tensor'}, dimensions={0} | all-to-all | bytes 131072 | tf_op jit(solution)/shard_map/all_to_all | solution.py:163
  32.1 0.6 %shard_map.66 = f32[4,512]{1,0:T(4,128)} custom-call(f32[128,128]{1,0:T(8,128)S(1)} %bitcast.17), custom_call_target="tpu_custom_call" | custom-call | tf_op jit(solution)/shard_map/pallas_call | solution.py:166
  (3 shorter events, 0.1 us)
Async XLA Ops:
  0.0 19.2 %copy-start.1 = (s32[1,4]{1,0:T(1,128)S(1)}, s32[1,4]{1,0:T(1,128)}, u32[]{:S(2)}) copy-start(s32[1,4]{1,0:T(1,128)} %doc_len.1) | copy-start | bytes 52
  0.0 19.2 %copy-start.2 = (s32[1,4]{1,0:T(1,128)S(1)}, s32[1,4]{1,0:T(1,128)}, u32[]{:S(2)}) copy-start(s32[1,4]{1,0:T(1,128)} %doc_owner.1) | copy-start | bytes 52
  0.6 18.5 %copy-start = (s32[2]{0:T(128)S(1)}, s32[2]{0:T(128)}, u32[]{:S(2)}) copy-start(s32[2]{0:T(128)} %pad_add_fusion.place) | copy-start | bytes 28
  6.5 1.7 %collective-permute-start = (f32[512,128]{1,0:T(8,128)S(1)}, f32[512,128]{1,0:T(8,128)S(1)}, u32[]{:S(2)}, u32[]{:S(2)}) collective-permute-start(f32[512,128]{1,0:T(8,128)S(1)} %get-tuple-element.8), channel_id=1, source_target_pairs={{0,1},{1,0},{2,3},{3,2},{4,5},{5,4},{6,7},{7,6},{8,9},{9,8},{10,11... | collective-permute-start | bytes 786440 | tf_op jit(solution)/shard_map/ppermute | solution.py:139
  8.2 7.7 %collective-permute-start.3 = (f32[128,128]{1,0:T(8,128)S(1)}, f32[128,128]{1,0:T(8,128)S(1)}, u32[]{:S(2)}, u32[]{:S(2)}) collective-permute-start(f32[128,128]{1,0:T(8,128)S(1)} %get-tuple-element.10), channel_id=1, source_target_pairs={{0,6},{1,7},{2,4},{3,5},{4,2},{5,3},{6,0},{7,1},{8,14},{9,15},{10,... | collective-permute-start | bytes 196616 | tf_op jit(solution)/shard_map/ppermute | solution.py:144
  13.3 5.9 %collective-permute-start.2 = (f32[128,128]{1,0:T(8,128)S(1)}, f32[128,128]{1,0:T(8,128)S(1)}, u32[]{:S(2)}, u32[]{:S(2)}) collective-permute-start(f32[128,128]{1,0:T(8,128)S(1)} %get-tuple-element.11), channel_id=1, source_target_pairs={{0,4},{1,5},{2,6},{3,7},{4,0},{5,1},{6,2},{7,3},{8,12},{9,13},{10,... | collective-permute-start | bytes 196616 | tf_op jit(solution)/shard_map/ppermute | solution.py:144
  13.3 5.9 %collective-permute-start.1 = (f32[128,128]{1,0:T(8,128)S(1)}, f32[128,128]{1,0:T(8,128)S(1)}, u32[]{:S(2)}, u32[]{:S(2)}) collective-permute-start(f32[128,128]{1,0:T(8,128)S(1)} %get-tuple-element.12), channel_id=1, source_target_pairs={{0,2},{1,3},{2,0},{3,1},{4,6},{5,7},{6,4},{7,5},{8,10},{9,11},{10,... | collective-permute-start | bytes 196616 | tf_op jit(solution)/shard_map/ppermute | solution.py:144

commit v2 on v1

v2 whole, which is shorter than its diff:
```python
import functools
import math
import jax
import jax.numpy as jnp
from jax import lax
from jax.experimental import pallas as pl
from jax.experimental.pallas import tpu as pltpu
from jax.sharding import PartitionSpec as P

NT = (((1,), (1,)), ((), ()))
TOP = 32767.0


def project(acts_hbm, grads_hbm, in_hbm, out_hbm, sums, held, weights, w_sems, sems):
    rank = in_hbm.shape[0]
    chunks, length, depth = held.shape
    hidden, width = acts_hbm.shape[1], grads_hbm.shape[1]
    rows = length // 4
    ahead = min(5, chunks)

    def copy(i):
        if i * depth < width:
            source = grads_hbm.at[:, pl.ds(i * depth, depth)]
        else:
            source = acts_hbm.at[:, pl.ds(i * depth - width, depth)]
        return pltpu.make_async_copy(source, held.at[i], sems.at[i])

    loads = (
        pltpu.make_async_copy(
            out_hbm, weights.at[pl.ds(rank, rank), pl.ds(0, width)], w_sems.at[0]
        ),
        pltpu.make_async_copy(
            in_hbm, weights.at[pl.ds(0, rank), pl.ds(width, hidden)], w_sems.at[1]
        ),
    )
    loads[0].start()
    copy(0).start()
    loads[1].start()
    for i in range(1, ahead):
        copy(i).start()
    weights[pl.ds(0, rank), pl.ds(0, width)] = jnp.zeros((rank, width), weights.dtype)
    weights[pl.ds(rank, rank), pl.ds(width, hidden)] = jnp.zeros((rank, hidden), weights.dtype)
    loads[0].wait()
    for i in range(chunks):
        if i * depth == width:
            loads[1].wait()
        copy(i).wait()
        if i + ahead < chunks:
            copy(i + ahead).start()
        block = weights[:, i * depth : (i + 1) * depth]
        for at in range(0, length, rows):
            part = held[i, pl.ds(at, rows), :]
            term = lax.dot_general(part, block, NT, preferred_element_type=jnp.float32)
            if i:
                sums[pl.ds(at, rows), :] += term
            else:
                sums[pl.ds(at, rows), :] = term


def code(at, sums, got, own, *sent):
    lanes, tokens = own.shape
    rank = lanes // 2
    pair = at[0] // 2
    kept = lax.rem(at[0], 2) * got.shape[0]

    def block(m):
        start = pl.multiple_of((pair ^ m) * tokens, tokens)
        mine = pl.ds(pl.multiple_of(kept + start, tokens), tokens)
        return (sums[mine, :] + got[pl.ds(start, tokens), :]).T

    own[...] = block(0)
    for m, out in enumerate(sent, 1):
        value = block(m)
        powers = []
        for side in range(2):
            part = value[side * rank : (side + 1) * rank]
            largest = jnp.max(jnp.abs(part), axis=0, keepdims=True)
            power = jnp.ceil(jnp.log2(jnp.maximum(largest, 1e-30)))
            steps = jnp.round(part * jnp.exp2(15.0 - power))
            steps = jnp.minimum(jnp.maximum(steps, -TOP), TOP).astype(jnp.int32)
            out[pl.ds(side * rank, rank), :] = steps.astype(jnp.int16)
            powers.append(power)
        row = lax.broadcasted_iota(jnp.int32, (out.shape[0] - lanes, tokens), 0)
        power = jnp.where(row == 0, powers[0], powers[1]).astype(jnp.int32)
        out[pl.ds(lanes, row.shape[0]), :] = power.astype(jnp.int16)


def outer(doc_len, doc_owner, at, own, *refs):
    *parts, out, sums, picked, other = refs
    lanes, tokens = own.shape
    docs = doc_len.shape[1]
    owners = out.shape[0]
    rank = lanes // 2
    half = rank // 2
    sides = [own[pl.ds(0, rank), :], own[pl.ds(rank, rank), :]]
    for part in parts:
        powers = part[pl.ds(lanes, part.shape[0] - lanes), :].astype(jnp.int32)
        scales = jnp.exp2(powers.astype(jnp.float32) - 15.0)
        for side in range(2):
            steps = part[pl.ds(side * rank, rank), :].astype(jnp.int32).astype(jnp.float32)
            sides[side] = sides[side] + steps * scales[side : side + 1]
    sums[...] = sides[1]
    zero = jnp.zeros((rank, tokens), jnp.float32)
    other[0, pl.ds(0, rank), :] = sides[0]
    other[0, pl.ds(rank, rank), :] = zero
    other[1, pl.ds(0, rank), :] = zero
    other[1, pl.ds(rank, rank), :] = sides[0]
    even = sums[pl.ds(0, half, stride=2), :]
    odd = sums[pl.ds(1, half, stride=2), :]
    start = lax.rem(at[0], 2) * (tokens * (len(parts) + 1)) + at[0] // 2 * tokens
    place = start + lax.broadcasted_iota(jnp.int32, even.shape, 1)
    starts = []
    start = jnp.int32(0)
    for k in range(docs):
        starts.append(start)
        start = start + doc_len[0, k]
    for o in range(owners):
        first, last = jnp.int32(0), jnp.int32(0)
        for k in range(docs):
            mine = doc_owner[0, k] == o
            first = jnp.where(mine, starts[k], first)
            last = jnp.where(mine, starts[k] + doc_len[0, k], last)
        live = (place >= first) & (place < last)
        picked[0, pl.ds(o * half, half), :] = jnp.where(live, even, 0.0)
        picked[1, pl.ds(o * half, half), :] = jnp.where(live, odd, 0.0)
    dot = functools.partial(
        lax.dot_general,
        dimension_numbers=NT,
        precision=lax.Precision.HIGHEST,
        preferred_element_type=jnp.float32,
    )
    grads = dot(picked[0], other[0]) + dot(picked[1], other[1])
    out[...] = grads.reshape(out.shape)


def collect(parts, out):
    seqs, width = out.shape
    lanes = parts.shape[1]
    blocks = width // lanes
    terms = parts.shape[0] // (seqs * blocks)
    for s in range(seqs):
        for c in range(blocks):
            block = parts[pl.ds(s * terms * blocks + c, terms, stride=blocks), :]
            out[pl.ds(s, 1), pl.ds(c * lanes, lanes)] = jnp.sum(block, axis=0, keepdims=True)


def on_device(acts, out_grads, proj_in, proj_out, doc_lengths, owner_map):
    owners = lax.axis_size("dp")
    split = lax.axis_size("tensor")
    length, hidden = acts.shape
    width = out_grads.shape[1]
    rank = proj_in.shape[1]
    lanes = 2 * rank
    depth = math.gcd(512, math.gcd(hidden, width))
    chunks = (hidden + width) // depth
    pairs = split // 2
    tokens = length // split
    half = length // 2
    vmem = pl.BlockSpec(memory_space=pltpu.VMEM)
    smem = pl.BlockSpec(memory_space=pltpu.SMEM)
    hbm = pl.BlockSpec(memory_space=pl.ANY)
    small = pltpu.CompilerParams(vmem_limit_bytes=8 << 20)

    at = lax.axis_index("tensor").astype(jnp.int32).reshape(1)
    sums = pl.pallas_call(
        project,
        out_shape=pltpu.VMEM((length, lanes), jnp.float32),
        in_specs=[hbm] * 4,
        out_specs=vmem,
        scratch_shapes=[
            pltpu.VMEM((chunks, length, depth), acts.dtype),
            pltpu.VMEM((lanes, hidden + width), proj_in.dtype),
            pltpu.SemaphoreType.DMA((2,)),
            pltpu.SemaphoreType.DMA((chunks,)),
        ],
        compiler_params=pltpu.CompilerParams(vmem_limit_bytes=56 << 20),
    )(acts, out_grads, proj_in.T, proj_out.T)
    sent = lax.dynamic_slice_in_dim(sums, (1 - at[0] % 2) * half, half, 0)
    got = lax.ppermute(sent, "tensor", [(i, i ^ 1) for i in range(split)])
    own, *coded = pl.pallas_call(
        code,
        out_shape=(pltpu.VMEM((lanes, tokens), jnp.float32),)
        + (pltpu.VMEM((lanes + 16, tokens), jnp.int16),) * (pairs - 1),
        in_specs=[smem, vmem, vmem],
        out_specs=(vmem,) * pairs,
        compiler_params=small,
    )(at, sums, got)
    parts = [None] * (pairs - 1)
    for m in range(1, pairs):
        parts[m - 1] = lax.ppermute(
            coded[m - 1], "tensor", [(i, i ^ (2 * m)) for i in range(split)]
        )
    grads = pl.pallas_call(
        outer,
        out_shape=pltpu.VMEM((owners, rank // 2, lanes), jnp.float32),
        in_specs=[smem] * 3 + [vmem] * pairs,
        out_specs=vmem,
        scratch_shapes=[
            pltpu.VMEM((rank, tokens), jnp.float32),
            pltpu.VMEM((2, owners * rank // 2, tokens), jnp.float32),
            pltpu.VMEM((2, lanes, tokens), jnp.float32),
        ],
        compiler_params=small,
    )(doc_lengths, owner_map, at, own, *parts)
    got = lax.all_to_all(
        grads.reshape(owners * rank // 2, lanes), ("dp", "tensor"), 0, 0, tiled=True
    )
    return pl.pallas_call(
        collect,
        out_shape=jax.ShapeDtypeStruct((owners, rank * rank // split), jnp.float32),
        in_specs=[vmem],
        out_specs=vmem,
        compiler_params=small,
    )(got)


def solution(mesh):
    in_specs = (
        P("dp", "tensor"),
        P("dp", "tensor"),
        P("tensor", None),
        P("tensor", None),
        P("dp", None),
        P("dp", None),
    )
    out_specs = P("dp", "tensor")
    return jax.shard_map(
        on_device, mesh=mesh, in_specs=in_specs, out_specs=out_specs, check_vma=False
    )
```

time: 32.8 us -> 29.6 us (0.902)
  blocking collectives: 11.9 us -> 9.97 us
  Pallas kernels: 7.36 us -> 6.36 us
  other arithmetic: 0.68 us -> 0 us
  waiting for transfers between devices: 6.4 us -> 6.91 us
    all_to_all x1, blocking collectives: 11.9 us -> 9.97 us  [on_device(): lax.all_to_all(grads.reshape(owners * rank // 2, lanes), ('dp', 'tensor')...]
    pallas_call x1 -> x2, Pallas kernels: 5.83 us -> 4.89 us  [the longest x1 4.72 us: on_device(): pl.pallas_call(project, out_shape=pltpu.VMEM((length, lanes), jnp.float32...]
    another operation x2 -> x0, other arithmetic: 0.65 us -> none  [the longest x1 0.63 us: on_device(): jnp.stack([core, core * (length // 2) + pair * tokens]).astype(jnp.int32)]
    ppermute x3, waiting for transfers between devices: 5.24 us -> 5.75 us  [on_device(): lax.ppermute(coded[m - 1], 'tensor', [(i, i ^ 2 * m) for i in range(split)])]
where the time goes in v2:
time: 29.6 us; the launch traced here: 29.4 us
  blocking collectives  9.97 us (34%)
  waiting for transfers between devices  6.91 us (23%)
  Pallas kernels  6.36 us (21%)
  starting transfers between devices  6.12 us (21%)
    all_to_all x1, blocking collectives, on_device(): lax.all_to_all(grads.reshape(owners * rank // 2, lanes), ('dp', 'tensor')...  9.97 us
    ppermute x3, waiting for transfers between devices, on_device(): lax.ppermute(coded[m - 1], 'tensor', [(i, i ^ 2 * m) for i in range(split)])  5.75 us
    ppermute x3, starting transfers between devices, on_device(): lax.ppermute(coded[m - 1], 'tensor', [(i, i ^ 2 * m) for i in range(split)])  5.6 us
    pallas_call x1, Pallas kernels, on_device(): pl.pallas_call(project, out_shape=pltpu.VMEM((length, lanes), jnp.float32...  4.72 us
    ppermute x1, waiting for transfers between devices, on_device(): got = lax.ppermute(sent, 'tensor', [(i, i ^ 1) for i in range(split)])  1.16 us
    pallas_call x1, Pallas kernels, on_device(): pl.pallas_call(outer, out_shape=pltpu.VMEM((owners, rank // 2, lanes), jn...  0.86 us
    pallas_call x1, Pallas kernels, on_device(): pl.pallas_call(collect, out_shape=jax.ShapeDtypeStruct((owners, rank * ra...  0.61 us
  transfers between devices with their start and end apart: 4, of which 3 were waited for; matrix products, arithmetic and copies ran while one was open for 0% of the time, Pallas kernels for 0%

profile of v2, /device:TPU:0, one launch (start us, length us, event | category | flops | bytes accessed | tf_op | source)
XLA Modules:
  0.0 29.4 jit_solution(11469896409647876553)
XLA Ops:
  0.0 0.0 copy-start.1
  0.0 0.0 copy-start
  0.0 4.7 %shard_map.64.sums = f32[1024,128]{1,0:T(8,128)S(1)} custom-call(bf16[1024,3584]{1,0:T(8,128)(2,1)} %acts_hbm.1, bf16[1024,1024]{1,0:T(8,128)(2,1)} %grads_hbm.1, bf16[64,3584]{1,0:T(8,128)(2,1)} %bitcast.7, bf16[64,1024]{1,0:T(8,128)(2,1)} %bitcast.8), custom_call_target="tpu_custom_call" | custom-call | tf_op jit(solution)/shard_map/pallas_call | solution.py:165
  4.8 0.5 %collective-permute-start = (f32[512,128]{1,0:T(8,128)S(1)}, f32[512,128]{1,0:T(8,128)S(1)}, u32[]{:S(2)}, u32[]{:S(2)}) collective-permute-start(f32[512,128]{1,0:T(8,128)S(1)} %constant_dynamic-slice_fusion), channel_id=1, source_target_pairs={{0,1},{1,0},{2,3},{3,2},{4,5},{5,4},{6,7},{7,6},{8,9},{9,8},{10,11... | collective-permute-start | bytes 786440 | tf_op jit(solution)/shard_map/ppermute | solution.py:179
  5.3 1.2 %collective-permute-done.got = f32[512,128]{1,0:T(8,128)S(1)} collective-permute-done((f32[512,128]{1,0:T(8,128)S(1)}, f32[512,128]{1,0:T(8,128)S(1)}, u32[]{:S(2)}, u32[]{:S(2)}) %collective-permute-start) | collective-permute-done | bytes 262176 | tf_op jit(solution)/shard_map/ppermute | solution.py:179
  6.5 0.2 shard_map.65
  6.6 3.0 %collective-permute-start.1 = (s16[144,128]{1,0:T(8,128)(2,1)S(1)}, s16[144,128]{1,0:T(8,128)(2,1)S(1)}, u32[]{:S(2)}, u32[]{:S(2)}) collective-permute-start(s16[144,128]{1,0:T(8,128)(2,1)S(1)} %get-tuple-element.10), channel_id=1, source_target_pairs={{0,2},{1,3},{2,0},{3,1},{4,6},{5,7},{6,4},{7,5},{8,10},{9,11},{10,... | collective-permute-start | bytes 110600 | tf_op jit(solution)/shard_map/ppermute | solution.py:190
  9.6 2.6 %collective-permute-start.2 = (s16[144,128]{1,0:T(8,128)(2,1)S(1)}, s16[144,128]{1,0:T(8,128)(2,1)S(1)}, u32[]{:S(2)}, u32[]{:S(2)}) collective-permute-start(s16[144,128]{1,0:T(8,128)(2,1)S(1)} %get-tuple-element.11), channel_id=1, source_target_pairs={{0,4},{1,5},{2,6},{3,7},{4,0},{5,1},{6,2},{7,3},{8,12},{9,13},{10,... | collective-permute-start | bytes 110600 | tf_op jit(solution)/shard_map/ppermute | solution.py:190
  12.2 0.0 collective-permute-start.3
  12.2 0.0 collective-permute-done.1.refs_0_
  12.2 3.0 %collective-permute-done.2.refs_1_ = s16[144,128]{1,0:T(8,128)(2,1)S(1)} collective-permute-done((s16[144,128]{1,0:T(8,128)(2,1)S(1)}, s16[144,128]{1,0:T(8,128)(2,1)S(1)}, u32[]{:S(2)}, u32[]{:S(2)}) %collective-permute-start.2) | collective-permute-done | bytes 36896 | tf_op jit(solution)/shard_map/ppermute | solution.py:190
  15.2 2.8 %collective-permute-done.3.refs_2_ = s16[144,128]{1,0:T(8,128)(2,1)S(1)} collective-permute-done((s16[144,128]{1,0:T(8,128)(2,1)S(1)}, s16[144,128]{1,0:T(8,128)(2,1)S(1)}, u32[]{:S(2)}, u32[]{:S(2)}) %collective-permute-start.3) | collective-permute-done | bytes 36896 | tf_op jit(solution)/shard_map/ppermute | solution.py:190
  18.0 0.0 copy-done.1
  18.0 0.0 copy-done
  18.0 0.9 %shard_map.66 = f32[4,32,128]{2,1,0:T(8,128)S(1)} custom-call(s32[1,4]{1,0:T(1,128)S(1)} %copy-done, s32[1,4]{1,0:T(1,128)S(1)} %copy-done.1, s32[1]{0:T(128)} %bitcast.at, f32[128,128]{1,0:T(8,128)S(1)} %get-tuple-element.9.own, s16[144,128]{1,0:T(8,128)(2,1)S(1)} %collective-permute-done.1.refs_0_, s16[144,128]{1,0:T(8,128)(2,1)S(1)} %collective-permute-done.2.refs_1_, ...), custom_call_target="tpu_custom_call" | custom-call | tf_op jit(solution)/shard_map/pallas_call | solution.py:193
  18.9 10.0 %all_to_all.11 = f32[32,4,128]{2,1,0:T(4,128)S(1)} all-to-all(f32[32,4,128]{2,1,0:T(4,128)S(1)} %bitcast.6), channel_id=1, replica_groups=mesh['dp'=4,'tensor'=8] {'dp','tensor'}, dimensions={0} | all-to-all | bytes 131072 | tf_op jit(solution)/shard_map/all_to_all | solution.py:205
  28.8 0.6 %shard_map.67 = f32[4,512]{1,0:T(4,128)} custom-call(f32[128,128]{1,0:T(8,128)S(1)} %bitcast.5), custom_call_target="tpu_custom_call" | custom-call | tf_op jit(solution)/shard_map/pallas_call | solution.py:208
  (1 shorter events, 0.0 us)
Async XLA Ops:
  0.0 18.0 %copy-start.1 = (s32[1,4]{1,0:T(1,128)S(1)}, s32[1,4]{1,0:T(1,128)}, u32[]{:S(2)}) copy-start(s32[1,4]{1,0:T(1,128)} %doc_owner.1) | copy-start | bytes 52
  0.0 18.0 %copy-start = (s32[1,4]{1,0:T(1,128)S(1)}, s32[1,4]{1,0:T(1,128)}, u32[]{:S(2)}) copy-start(s32[1,4]{1,0:T(1,128)} %doc_len.1) | copy-start | bytes 52
  4.8 1.7 %collective-permute-start = (f32[512,128]{1,0:T(8,128)S(1)}, f32[512,128]{1,0:T(8,128)S(1)}, u32[]{:S(2)}, u32[]{:S(2)}) collective-permute-start(f32[512,128]{1,0:T(8,128)S(1)} %constant_dynamic-slice_fusion), channel_id=1, source_target_pairs={{0,1},{1,0},{2,3},{3,2},{4,5},{5,4},{6,7},{7,6},{8,9},{9,8},{10,11... | collective-permute-start | bytes 786440 | tf_op jit(solution)/shard_map/ppermute | solution.py:179
  6.6 5.6 %collective-permute-start.1 = (s16[144,128]{1,0:T(8,128)(2,1)S(1)}, s16[144,128]{1,0:T(8,128)(2,1)S(1)}, u32[]{:S(2)}, u32[]{:S(2)}) collective-permute-start(s16[144,128]{1,0:T(8,128)(2,1)S(1)} %get-tuple-element.10), channel_id=1, source_target_pairs={{0,2},{1,3},{2,0},{3,1},{4,6},{5,7},{6,4},{7,5},{8,10},{9,11},{10,... | collective-permute-start | bytes 110600 | tf_op jit(solution)/shard_map/ppermute | solution.py:190
  9.6 5.6 %collective-permute-start.2 = (s16[144,128]{1,0:T(8,128)(2,1)S(1)}, s16[144,128]{1,0:T(8,128)(2,1)S(1)}, u32[]{:S(2)}, u32[]{:S(2)}) collective-permute-start(s16[144,128]{1,0:T(8,128)(2,1)S(1)} %get-tuple-element.11), channel_id=1, source_target_pairs={{0,4},{1,5},{2,6},{3,7},{4,0},{5,1},{6,2},{7,3},{8,12},{9,13},{10,... | collective-permute-start | bytes 110600 | tf_op jit(solution)/shard_map/ppermute | solution.py:190
  12.2 5.8 %collective-permute-start.3 = (s16[144,128]{1,0:T(8,128)(2,1)S(1)}, s16[144,128]{1,0:T(8,128)(2,1)S(1)}, u32[]{:S(2)}, u32[]{:S(2)}) collective-permute-start(s16[144,128]{1,0:T(8,128)(2,1)S(1)} %get-tuple-element.12), channel_id=1, source_target_pairs={{0,6},{1,7},{2,4},{3,5},{4,2},{5,3},{6,0},{7,1},{8,14},{9,15},{10,... | collective-permute-start | bytes 110600 | tf_op jit(solution)/shard_map/ppermute | solution.py:190

commit v3 on v2

--- a/solution.py
+++ b/solution.py
@@ -57,7 +57,7 @@
                 sums[pl.ds(at, rows), :] = term
 
 
-def code(at, sums, got, own, *sent):
+def code(order, at, sums, got, own, *sent):
     lanes, tokens = own.shape
     rank = lanes // 2
     pair = at[0] // 2
@@ -69,7 +69,7 @@
         return (sums[mine, :] + got[pl.ds(start, tokens), :]).T
 
     own[...] = block(0)
-    for m, out in enumerate(sent, 1):
+    for m, out in zip(order, sent):
         value = block(m)
         powers = []
         for side in range(2):
@@ -85,10 +85,34 @@
         out[pl.ds(lanes, row.shape[0]), :] = power.astype(jnp.int16)
 
 
-def outer(doc_len, doc_owner, at, own, *refs):
+def members(pairs, doc_len, doc_owner, at, lives):
+    owners, tokens = lives.shape
+    docs = doc_len.shape[1]
+    core, pair = lax.rem(at[0], 2), at[0] // 2
+    first_token = (core * pairs + pair) * tokens
+    place = first_token + lax.broadcasted_iota(jnp.int32, (1, tokens), 1)
+    starts = []
+    start = jnp.int32(0)
+    for k in range(docs):
+        starts.append(start)
+        start = start + doc_len[0, k]
+    for o in range(owners):
+        first, last = jnp.int32(0), jnp.int32(0)
+        for k in range(docs):
+            mine = doc_owner[0, k] == o
+            first = jnp.where(mine, starts[k], first)
+            last = jnp.where(mine, starts[k] + doc_len[0, k], last)
+        lives[pl.ds(o, 1), :] = ((place >= first) & (place < last)).astype(jnp.float32)
+
+
+def cut(value):
+    high = value.astype(jnp.bfloat16)
+    return high, (value - high.astype(jnp.float32)).astype(jnp.bfloat16)
+
+
+def outer(lives, own, *refs):
     *parts, out, sums, picked, other = refs
     lanes, tokens = own.shape
-    docs = doc_len.shape[1]
     owners = out.shape[0]
     rank = lanes // 2
     half = rank // 2
@@ -100,36 +124,22 @@
             steps = part[pl.ds(side * rank, rank), :].astype(jnp.int32).astype(jnp.float32)
             sides[side] = sides[side] + steps * scales[side : side + 1]
     sums[...] = sides[1]
-    zero = jnp.zeros((rank, tokens), jnp.float32)
-    other[0, pl.ds(0, rank), :] = sides[0]
-    other[0, pl.ds(rank, rank), :] = zero
-    other[1, pl.ds(0, rank), :] = zero
-    other[1, pl.ds(rank, rank), :] = sides[0]
-    even = sums[pl.ds(0, half, stride=2), :]
-    odd = sums[pl.ds(1, half, stride=2), :]
-    start = lax.rem(at[0], 2) * (tokens * (len(parts) + 1)) + at[0] // 2 * tokens
-    place = start + lax.broadcasted_iota(jnp.int32, even.shape, 1)
-    starts = []
-    start = jnp.int32(0)
-    for k in range(docs):
-        starts.append(start)
-        start = start + doc_len[0, k]
+    high, low = cut(sides[0])
+    other[...] = jnp.zeros(other.shape, other.dtype)
+    for side in range(2):
+        for term, piece in enumerate((high, low, high)):
+            columns = pl.ds((2 * term + side) * tokens, tokens)
+            other[pl.ds(side * rank, rank), columns] = piece
+    high, low = zip(*(cut(sums[pl.ds(side, half, stride=2), :]) for side in range(2)))
     for o in range(owners):
-        first, last = jnp.int32(0), jnp.int32(0)
-        for k in range(docs):
-            mine = doc_owner[0, k] == o
-            first = jnp.where(mine, starts[k], first)
-            last = jnp.where(mine, starts[k] + doc_len[0, k], last)
-        live = (place >= first) & (place < last)
-        picked[0, pl.ds(o * half, half), :] = jnp.where(live, even, 0.0)
-        picked[1, pl.ds(o * half, half), :] = jnp.where(live, odd, 0.0)
-    dot = functools.partial(
-        lax.dot_general,
-        dimension_numbers=NT,
-        precision=lax.Precision.HIGHEST,
-        preferred_element_type=jnp.float32,
-    )
-    grads = dot(picked[0], other[0]) + dot(picked[1], other[1])
+        live = jnp.broadcast_to(lives[pl.ds(o, 1), :], high[0].shape) > 0
+        for side in range(2):
+            for term, piece in enumerate((high, high, low)):
+                columns = pl.ds((2 * term + side) * tokens, tokens)
+                picked[pl.ds(o * half, half), columns] = jnp.where(
+                    live, piece[side], jnp.zeros((), piece[side].dtype)
+                )
+    grads = lax.dot_general(picked[...], other[...], NT, preferred_element_type=jnp.float32)
     out[...] = grads.reshape(out.shape)
 
 
@@ -177,31 +187,38 @@
     )(acts, out_grads, proj_in.T, proj_out.T)
     sent = lax.dynamic_slice_in_dim(sums, (1 - at[0] % 2) * half, half, 0)
     got = lax.ppermute(sent, "tensor", [(i, i ^ 1) for i in range(split)])
+    order = tuple(range(1, pairs))
     own, *coded = pl.pallas_call(
-        code,
+        functools.partial(code, order),
         out_shape=(pltpu.VMEM((lanes, tokens), jnp.float32),)
         + (pltpu.VMEM((lanes + 16, tokens), jnp.int16),) * (pairs - 1),
         in_specs=[smem, vmem, vmem],
         out_specs=(vmem,) * pairs,
         compiler_params=small,
     )(at, sums, got)
-    parts = [None] * (pairs - 1)
-    for m in range(1, pairs):
-        parts[m - 1] = lax.ppermute(
-            coded[m - 1], "tensor", [(i, i ^ (2 * m)) for i in range(split)]
-        )
+    parts = [
+        lax.ppermute(block, "tensor", [(i, i ^ (2 * m)) for i in range(split)])
+        for m, block in zip(order, coded)
+    ]
+    lives = pl.pallas_call(
+        functools.partial(members, pairs),
+        out_shape=pltpu.VMEM((owners, tokens), jnp.float32),
+        in_specs=[smem] * 3,
+        out_specs=vmem,
+        compiler_params=small,
+    )(doc_lengths, owner_map, at)
     grads = pl.pallas_call(
         outer,
         out_shape=pltpu.VMEM((owners, rank // 2, lanes), jnp.float32),
-        in_specs=[smem] * 3 + [vmem] * pairs,
+        in_specs=[vmem] * (pairs + 1),
         out_specs=vmem,
         scratch_shapes=[
             pltpu.VMEM((rank, tokens), jnp.float32),
-            pltpu.VMEM((2, owners * rank // 2, tokens), jnp.float32),
-            pltpu.VMEM((2, lanes, tokens), jnp.float32),
+            pltpu.VMEM((owners * rank // 2, 6 * tokens), jnp.bfloat16),
+            pltpu.VMEM((lanes, 6 * tokens), jnp.bfloat16),
         ],
         compiler_params=small,
-    )(doc_lengths, owner_map, at, own, *parts)
+    )(lives, own, *parts)
     got = lax.all_to_all(
         grads.reshape(owners * rank // 2, lanes), ("dp", "tensor"), 0, 0, tiled=True
     )

time: 29.6 us -> 29 us (0.980)
  waiting for transfers between devices: 6.91 us -> 6.32 us
    pallas_call x1, Pallas kernels: 0.86 us -> 0.25 us  [on_device(): pl.pallas_call(outer, out_shape=pltpu.VMEM((owners, rank // 2, lanes), jn...]
    ppermute x3, waiting for transfers between devices: 5.75 us -> 5.16 us  [on_device(): lax.ppermute(block, 'tensor', [(i, i ^ 2 * m) for i in range(split)])]
    pallas_call x1 -> x2, Pallas kernels: 0.17 us -> 0.75 us  [the longest x1 0.57 us: on_device(): pl.pallas_call(functools.partial(members, pairs), out_shape=pltpu.VMEM((o...]
  transfers between devices with their start and end apart: 4 -> 4, of which waited for: 3 -> 3; matrix products, arithmetic and copies ran while one was open for 0% -> 0% of each run, Pallas kernels for 0% -> 2%
where the time goes in v3:
time: 29 us; the launch traced here: 28.8 us
  blocking collectives  9.97 us (34%)
  Pallas kernels  6.33 us (22%)
  waiting for transfers between devices  6.32 us (22%)
  starting transfers between devices  6.12 us (21%)
    all_to_all x1, blocking collectives, on_device(): lax.all_to_all(grads.reshape(owners * rank // 2, lanes), ('dp', 'tensor')...  9.97 us
    ppermute x3, starting transfers between devices, on_device(): lax.ppermute(block, 'tensor', [(i, i ^ 2 * m) for i in range(split)])  5.6 us
    ppermute x3, waiting for transfers between devices, on_device(): lax.ppermute(block, 'tensor', [(i, i ^ 2 * m) for i in range(split)])  5.16 us
    pallas_call x1, Pallas kernels, on_device(): pl.pallas_call(project, out_shape=pltpu.VMEM((length, lanes), jnp.float32...  4.72 us
    ppermute x1, waiting for transfers between devices, on_device(): got = lax.ppermute(sent, 'tensor', [(i, i ^ 1) for i in range(split)])  1.16 us
    pallas_call x1, Pallas kernels, on_device(): pl.pallas_call(collect, out_shape=jax.ShapeDtypeStruct((owners, rank * ra...  0.61 us
  transfers between devices with their start and end apart: 4, of which 3 were waited for; matrix products, arithmetic and copies ran while one was open for 0% of the time, Pallas kernels for 2%

profile of v3, /device:TPU:0, one launch (start us, length us, event | category | flops | bytes accessed | tf_op | source)
XLA Modules:
  0.0 28.8 jit_solution(847224087951644077)
XLA Ops:
  0.0 0.0 copy-start
  0.0 0.0 copy-start.1
  0.0 4.7 %shard_map.65.sums = f32[1024,128]{1,0:T(8,128)S(1)} custom-call(bf16[1024,3584]{1,0:T(8,128)(2,1)} %acts_hbm.1, bf16[1024,1024]{1,0:T(8,128)(2,1)} %grads_hbm.1, bf16[64,3584]{1,0:T(8,128)(2,1)} %bitcast.7, bf16[64,1024]{1,0:T(8,128)(2,1)} %bitcast.8), custom_call_target="tpu_custom_call" | custom-call | tf_op jit(solution)/shard_map/pallas_call | solution.py:175
  4.8 0.5 %collective-permute-start = (f32[512,128]{1,0:T(8,128)S(1)}, f32[512,128]{1,0:T(8,128)S(1)}, u32[]{:S(2)}, u32[]{:S(2)}) collective-permute-start(f32[512,128]{1,0:T(8,128)S(1)} %constant_dynamic-slice_fusion), channel_id=1, source_target_pairs={{0,1},{1,0},{2,3},{3,2},{4,5},{5,4},{6,7},{7,6},{8,9},{9,8},{10,11... | collective-permute-start | bytes 786440 | tf_op jit(solution)/shard_map/ppermute | solution.py:189
  5.3 1.2 %collective-permute-done.got = f32[512,128]{1,0:T(8,128)S(1)} collective-permute-done((f32[512,128]{1,0:T(8,128)S(1)}, f32[512,128]{1,0:T(8,128)S(1)}, u32[]{:S(2)}, u32[]{:S(2)}) %collective-permute-start) | collective-permute-done | bytes 262176 | tf_op jit(solution)/shard_map/ppermute | solution.py:189
  6.5 0.2 shard_map.66
  6.6 3.0 %collective-permute-start.1 = (s16[144,128]{1,0:T(8,128)(2,1)S(1)}, s16[144,128]{1,0:T(8,128)(2,1)S(1)}, u32[]{:S(2)}, u32[]{:S(2)}) collective-permute-start(s16[144,128]{1,0:T(8,128)(2,1)S(1)} %get-tuple-element.10), channel_id=1, source_target_pairs={{0,2},{1,3},{2,0},{3,1},{4,6},{5,7},{6,4},{7,5},{8,10},{9,11},{10,... | collective-permute-start | bytes 110600 | tf_op jit(solution)/shard_map/ppermute | solution.py:200
  9.6 2.6 %collective-permute-start.2 = (s16[144,128]{1,0:T(8,128)(2,1)S(1)}, s16[144,128]{1,0:T(8,128)(2,1)S(1)}, u32[]{:S(2)}, u32[]{:S(2)}) collective-permute-start(s16[144,128]{1,0:T(8,128)(2,1)S(1)} %get-tuple-element.11), channel_id=1, source_target_pairs={{0,4},{1,5},{2,6},{3,7},{4,0},{5,1},{6,2},{7,3},{8,12},{9,13},{10,... | collective-permute-start | bytes 110600 | tf_op jit(solution)/shard_map/ppermute | solution.py:200
  12.2 0.0 collective-permute-start.3
  12.2 0.0 copy-done
  12.2 0.0 copy-done.1
  12.2 0.6 %shard_map.64.lives = f32[4,128]{1,0:T(4,128)S(1)} custom-call(s32[1,4]{1,0:T(1,128)S(1)} %copy-done, s32[1,4]{1,0:T(1,128)S(1)} %copy-done.1, s32[1]{0:T(128)} %bitcast.at), custom_call_target="tpu_custom_call" | custom-call | tf_op jit(solution)/shard_map/pallas_call | solution.py:203
  12.8 0.0 collective-permute-done.1.refs_0_
  12.8 2.4 %collective-permute-done.2.refs_1_ = s16[144,128]{1,0:T(8,128)(2,1)S(1)} collective-permute-done((s16[144,128]{1,0:T(8,128)(2,1)S(1)}, s16[144,128]{1,0:T(8,128)(2,1)S(1)}, u32[]{:S(2)}, u32[]{:S(2)}) %collective-permute-start.2) | collective-permute-done | bytes 36896 | tf_op jit(solution)/shard_map/ppermute | solution.py:200
  15.2 2.8 %collective-permute-done.3.refs_2_ = s16[144,128]{1,0:T(8,128)(2,1)S(1)} collective-permute-done((s16[144,128]{1,0:T(8,128)(2,1)S(1)}, s16[144,128]{1,0:T(8,128)(2,1)S(1)}, u32[]{:S(2)}, u32[]{:S(2)}) %collective-permute-start.3) | collective-permute-done | bytes 36896 | tf_op jit(solution)/shard_map/ppermute | solution.py:200
  18.0 0.2 shard_map.67
  18.2 10.0 %all_to_all.11 = f32[32,4,128]{2,1,0:T(4,128)S(1)} all-to-all(f32[32,4,128]{2,1,0:T(4,128)S(1)} %bitcast.6), channel_id=1, replica_groups=mesh['dp'=4,'tensor'=8] {'dp','tensor'}, dimensions={0} | all-to-all | bytes 131072 | tf_op jit(solution)/shard_map/all_to_all | solution.py:222
  28.2 0.6 %shard_map.68 = f32[4,512]{1,0:T(4,128)} custom-call(f32[128,128]{1,0:T(8,128)S(1)} %bitcast.5), custom_call_target="tpu_custom_call" | custom-call | tf_op jit(solution)/shard_map/pallas_call | solution.py:225
  (1 shorter events, 0.0 us)
Async XLA Ops:
  0.0 12.2 %copy-start = (s32[1,4]{1,0:T(1,128)S(1)}, s32[1,4]{1,0:T(1,128)}, u32[]{:S(2)}) copy-start(s32[1,4]{1,0:T(1,128)} %doc_len.1) | copy-start | bytes 52
  0.0 12.2 %copy-start.1 = (s32[1,4]{1,0:T(1,128)S(1)}, s32[1,4]{1,0:T(1,128)}, u32[]{:S(2)}) copy-start(s32[1,4]{1,0:T(1,128)} %doc_owner.1) | copy-start | bytes 52
  4.8 1.7 %collective-permute-start = (f32[512,128]{1,0:T(8,128)S(1)}, f32[512,128]{1,0:T(8,128)S(1)}, u32[]{:S(2)}, u32[]{:S(2)}) collective-permute-start(f32[512,128]{1,0:T(8,128)S(1)} %constant_dynamic-slice_fusion), channel_id=1, source_target_pairs={{0,1},{1,0},{2,3},{3,2},{4,5},{5,4},{6,7},{7,6},{8,9},{9,8},{10,11... | collective-permute-start | bytes 786440 | tf_op jit(solution)/shard_map/ppermute | solution.py:189
  6.6 6.2 %collective-permute-start.1 = (s16[144,128]{1,0:T(8,128)(2,1)S(1)}, s16[144,128]{1,0:T(8,128)(2,1)S(1)}, u32[]{:S(2)}, u32[]{:S(2)}) collective-permute-start(s16[144,128]{1,0:T(8,128)(2,1)S(1)} %get-tuple-element.10), channel_id=1, source_target_pairs={{0,2},{1,3},{2,0},{3,1},{4,6},{5,7},{6,4},{7,5},{8,10},{9,11},{10,... | collective-permute-start | bytes 110600 | tf_op jit(solution)/shard_map/ppermute | solution.py:200
  9.6 5.6 %collective-permute-start.2 = (s16[144,128]{1,0:T(8,128)(2,1)S(1)}, s16[144,128]{1,0:T(8,128)(2,1)S(1)}, u32[]{:S(2)}, u32[]{:S(2)}) collective-permute-start(s16[144,128]{1,0:T(8,128)(2,1)S(1)} %get-tuple-element.11), channel_id=1, source_target_pairs={{0,4},{1,5},{2,6},{3,7},{4,0},{5,1},{6,2},{7,3},{8,12},{9,13},{10,... | collective-permute-start | bytes 110600 | tf_op jit(solution)/shard_map/ppermute | solution.py:200
  12.2 5.8 %collective-permute-start.3 = (s16[144,128]{1,0:T(8,128)(2,1)S(1)}, s16[144,128]{1,0:T(8,128)(2,1)S(1)}, u32[]{:S(2)}, u32[]{:S(2)}) collective-permute-start(s16[144,128]{1,0:T(8,128)(2,1)S(1)} %get-tuple-element.12), channel_id=1, source_target_pairs={{0,6},{1,7},{2,4},{3,5},{4,2},{5,3},{6,0},{7,1},{8,14},{9,15},{10,... | collective-permute-start | bytes 110600 | tf_op jit(solution)/shard_map/ppermute | solution.py:200

commit v4 on v3

--- a/solution.py
+++ b/solution.py
@@ -11,20 +11,39 @@
 TOP = 32767.0
 
 
-def project(acts_hbm, grads_hbm, in_hbm, out_hbm, sums, held, weights, w_sems, sems):
+def add_product(out, first, left, right):
+    rows = left.shape[0] // 2
+    for at in range(0, left.shape[0], rows):
+        part = left[pl.ds(at, rows), :]
+        term = lax.dot_general(part, right, NT, preferred_element_type=jnp.float32)
+        if first:
+            out[pl.ds(at, rows), :] = term
+        else:
+            out[pl.ds(at, rows), :] += term
+
+
+def columns_of(acts_hbm, grads_hbm, base, half, depth, i, to, sem):
+    rows = pl.ds(pl.multiple_of(base, half), half)
+    width = grads_hbm.shape[1]
+    if i * depth < width:
+        source = grads_hbm.at[rows, pl.ds(i * depth, depth)]
+    else:
+        source = acts_hbm.at[rows, pl.ds(i * depth - width, depth)]
+    return pltpu.make_async_copy(source, to, sem)
+
+
+def project_sent(at, acts_hbm, grads_hbm, in_hbm, out_hbm, sent, weights, early, held, w_sems, sems):
     rank = in_hbm.shape[0]
-    chunks, length, depth = held.shape
+    chunks, half, depth = held.shape
     hidden, width = acts_hbm.shape[1], grads_hbm.shape[1]
-    rows = length // 4
-    ahead = min(5, chunks)
-
-    def copy(i):
-        if i * depth < width:
-            source = grads_hbm.at[:, pl.ds(i * depth, depth)]
-        else:
-            source = acts_hbm.at[:, pl.ds(i * depth - width, depth)]
-        return pltpu.make_async_copy(source, held.at[i], sems.at[i])
-
+    core = lax.rem(at[0], 2)
+    copies = [
+        columns_of(acts_hbm, grads_hbm, (1 - core) * half, half, depth, i, held.at[i], sems.at[i])
+        for i in range(chunks)
+    ] + [
+        columns_of(acts_hbm, grads_hbm, core * half, half, depth, i, early.at[i], sems.at[chunks + i])
+        for i in range(early.shape[0])
+    ]
     loads = (
         pltpu.make_async_copy(
             out_hbm, weights.at[pl.ds(rank, rank), pl.ds(0, width)], w_sems.at[0]
@@ -34,39 +53,53 @@
         ),
     )
     loads[0].start()
-    copy(0).start()
+    copies[0].start()
     loads[1].start()
-    for i in range(1, ahead):
-        copy(i).start()
+    for copy in copies[1:8]:
+        copy.start()
     weights[pl.ds(0, rank), pl.ds(0, width)] = jnp.zeros((rank, width), weights.dtype)
     weights[pl.ds(rank, rank), pl.ds(width, hidden)] = jnp.zeros((rank, hidden), weights.dtype)
     loads[0].wait()
     for i in range(chunks):
         if i * depth == width:
             loads[1].wait()
-        copy(i).wait()
-        if i + ahead < chunks:
-            copy(i + ahead).start()
-        block = weights[:, i * depth : (i + 1) * depth]
-        for at in range(0, length, rows):
-            part = held[i, pl.ds(at, rows), :]
-            term = lax.dot_general(part, block, NT, preferred_element_type=jnp.float32)
-            if i:
-                sums[pl.ds(at, rows), :] += term
-            else:
-                sums[pl.ds(at, rows), :] = term
-
-
-def code(order, at, sums, got, own, *sent):
+        copies[i].wait()
+        if i + 8 < len(copies):
+            copies[i + 8].start()
+        add_product(sent, i == 0, held.at[i], weights[:, i * depth : (i + 1) * depth])
+    for copy in copies[chunks:]:
+        copy.wait()
+
+
+def project_kept(at, acts_hbm, grads_hbm, weights, early, kept, held, sems):
+    rest, half, depth = held.shape
+    ready = early.shape[0]
+    core = lax.rem(at[0], 2)
+    copies = [
+        columns_of(acts_hbm, grads_hbm, core * half, half, depth, ready + i, held.at[i], sems.at[i])
+        for i in range(rest)
+    ]
+    for copy in copies[:8]:
+        copy.start()
+    for i in range(ready + rest):
+        if i < ready:
+            left = early.at[i]
+        else:
+            left = held.at[i - ready]
+            copies[i - ready].wait()
+            if i - ready + 8 < rest:
+                copies[i - ready + 8].start()
+        add_product(kept, i == 0, left, weights[:, i * depth : (i + 1) * depth])
+
+
+def code(order, at, kept, got, own, *sent):
     lanes, tokens = own.shape
     rank = lanes // 2
     pair = at[0] // 2
-    kept = lax.rem(at[0], 2) * got.shape[0]
 
     def block(m):
-        start = pl.multiple_of((pair ^ m) * tokens, tokens)
-        mine = pl.ds(pl.multiple_of(kept + start, tokens), tokens)
-        return (sums[mine, :] + got[pl.ds(start, tokens), :]).T
+        rows = pl.ds(pl.multiple_of((pair ^ m) * tokens, tokens), tokens)
+        return (kept[rows, :] + got[rows, :]).T
 
     own[...] = block(0)
     for m, out in zip(order, sent):
@@ -143,17 +176,6 @@
     out[...] = grads.reshape(out.shape)
 
 
-def collect(parts, out):
-    seqs, width = out.shape
-    lanes = parts.shape[1]
-    blocks = width // lanes
-    terms = parts.shape[0] // (seqs * blocks)
-    for s in range(seqs):
-        for c in range(blocks):
-            block = parts[pl.ds(s * terms * blocks + c, terms, stride=blocks), :]
-            out[pl.ds(s, 1), pl.ds(c * lanes, lanes)] = jnp.sum(block, axis=0, keepdims=True)
-
-
 def on_device(acts, out_grads, proj_in, proj_out, doc_lengths, owner_map):
     owners = lax.axis_size("dp")
     split = lax.axis_size("tensor")
@@ -172,21 +194,48 @@
     small = pltpu.CompilerParams(vmem_limit_bytes=8 << 20)
 
     at = lax.axis_index("tensor").astype(jnp.int32).reshape(1)
-    sums = pl.pallas_call(
-        project,
-        out_shape=pltpu.VMEM((length, lanes), jnp.float32),
-        in_specs=[hbm] * 4,
+    acts, out_grads, w_in, w_out = (
+        pltpu.with_memory_space_constraint(array, pltpu.HBM)
+        for array in (acts, out_grads, proj_in.T, proj_out.T)
+    )
+    ready = min(3, chunks - 1)
+    sums = pltpu.VMEM((half, lanes), jnp.float32)
+    medium = pltpu.CompilerParams(vmem_limit_bytes=16 << 20)
+    cost = pl.CostEstimate(
+        flops=2 * half * lanes * (hidden + width),
+        bytes_accessed=2 * half * (hidden + width),
+        transcendentals=0,
+    )
+    sent, weights, early = pl.pallas_call(
+        project_sent,
+        out_shape=(
+            sums,
+            pltpu.VMEM((lanes, hidden + width), proj_in.dtype),
+            pltpu.VMEM((ready, half, depth), acts.dtype),
+        ),
+        in_specs=[smem] + [hbm] * 4,
+        out_specs=(vmem,) * 3,
+        scratch_shapes=[
+            pltpu.VMEM((chunks, half, depth), acts.dtype),
+            pltpu.SemaphoreType.DMA((2,)),
+            pltpu.SemaphoreType.DMA((chunks + ready,)),
+        ],
+        compiler_params=medium,
+        cost_estimate=cost,
+    )(at, acts, out_grads, w_in, w_out)
+    got = lax.ppermute(sent, "tensor", [(i, i ^ 1) for i in range(split)])
+    kept = pl.pallas_call(
+        project_kept,
+        out_shape=sums,
+        in_specs=[smem, hbm, hbm, vmem, vmem],
         out_specs=vmem,
         scratch_shapes=[
-            pltpu.VMEM((chunks, length, depth), acts.dtype),
-            pltpu.VMEM((lanes, hidden + width), proj_in.dtype),
-            pltpu.SemaphoreType.DMA((2,)),
-            pltpu.SemaphoreType.DMA((chunks,)),
+            pltpu.VMEM((chunks - ready, half, depth), acts.dtype),
+            pltpu.SemaphoreType.DMA((chunks - ready,)),
         ],
-        compiler_params=pltpu.CompilerParams(vmem_limit_bytes=56 << 20),
-    )(acts, out_grads, proj_in.T, proj_out.T)
-    sent = lax.dynamic_slice_in_dim(sums, (1 - at[0] % 2) * half, half, 0)
-    got = lax.ppermute(sent, "tensor", [(i, i ^ 1) for i in range(split)])
+        compiler_params=medium,
+        cost_estimate=cost,
+    )(at, acts, out_grads, weights, early)
     order = tuple(range(1, pairs))
     own, *coded = pl.pallas_call(
         functools.partial(code, order),
@@ -195,7 +244,7 @@
         in_specs=[smem, vmem, vmem],
         out_specs=(vmem,) * pairs,
         compiler_params=small,
-    )(at, sums, got)
+    )(at, kept, got)
     parts = [
         lax.ppermute(block, "tensor", [(i, i ^ (2 * m)) for i in range(split)])
         for m, block in zip(order, coded)
@@ -222,13 +271,8 @@
     got = lax.all_to_all(
         grads.reshape(owners * rank // 2, lanes), ("dp", "tensor"), 0, 0, tiled=True
     )
-    return pl.pallas_call(
-        collect,
-        out_shape=jax.ShapeDtypeStruct((owners, rank * rank // split), jnp.float32),
-        in_specs=[vmem],
-        out_specs=vmem,
-        compiler_params=small,
-    )(got)
+    blocks = rank * rank // (split * lanes)
+    return jnp.sum(got.reshape(owners, split, blocks, lanes), 1).reshape(owners, blocks * lanes)
 
 
 def solution(mesh):

time: 29 us -> 28.8 us (level)
  waiting for transfers between devices: 6.32 us -> 5.16 us
  Pallas kernels: 6.33 us -> 6.98 us
  local copies, waits for them, and re-layouts: 0.03 us -> 0.61 us
  starting transfers between devices: 6.12 us -> 5.78 us
    ppermute x1, waiting for transfers between devices: 1.16 us -> 0.01 us  [on_device(): got = lax.ppermute(sent, 'tensor', [(i, i ^ 1) for i in range(split)])]
    pallas_call x2, Pallas kernels: 5.33 us -> 5.98 us  [the longest x1 3.61 us: on_device(): pl.pallas_call(project_sent, out_shape=(sums, pltpu.VMEM((lanes, hidden +...]
    unnamed x4 -> x5, local copies, waits for them, and re-layouts: 0.01 us -> 0.61 us
    ppermute x3, starting transfers between devices: 5.6 us -> 5.24 us  [on_device(): lax.ppermute(block, 'tensor', [(i, i ^ 2 * m) for i in range(split)])]
  transfers between devices with their start and end apart: 4 -> 4, of which waited for: 3 -> 2; matrix products, arithmetic and copies ran while one was open for 0% -> 0% of each run, Pallas kernels for 2% -> 10%
where the time goes in v4:
time: 28.8 us; the launch traced here: 28.6 us
  blocking collectives  10 us (35%)
  Pallas kernels  6.98 us (24%)
  starting transfers between devices  5.78 us (20%)
  waiting for transfers between devices  5.16 us (18%)
  local copies, waits for them, and re-layouts  0.61 us (2%)
    all_to_all x1, blocking collectives, on_device(): lax.all_to_all(grads.reshape(owners * rank // 2, lanes), ('dp', 'tensor')...  10 us
    ppermute x3, starting transfers between devices, on_device(): lax.ppermute(block, 'tensor', [(i, i ^ 2 * m) for i in range(split)])  5.24 us
    ppermute x3, waiting for transfers between devices, on_device(): lax.ppermute(block, 'tensor', [(i, i ^ 2 * m) for i in range(split)])  5.16 us
    pallas_call x1, Pallas kernels, on_device(): pl.pallas_call(project_sent, out_shape=(sums, pltpu.VMEM((lanes, hidden +...  3.61 us
    pallas_call x1, Pallas kernels, on_device(): pl.pallas_call(project_kept, out_shape=sums, in_specs=[smem, hbm, hbm, vm...  2.36 us
    unnamed x5, local copies, waits for them, and re-layouts  0.61 us
  transfers between devices with their start and end apart: 4, of which 2 were waited for; matrix products, arithmetic and copies ran while one was open for 0% of the time, Pallas kernels for 10%

profile of v4, /device:TPU:0, one launch (start us, length us, event | category | flops | bytes accessed | tf_op | source)
XLA Modules:
  0.0 28.6 jit_solution(10267530947134726071)
XLA Ops:
  0.0 3.6 %shard_map.65 = (f32[512,128]{1,0:T(8,128)S(1)}, bf16[128,4608]{1,0:T(8,128)(2,1)S(1)}, bf16[3,512,512]{2,1,0:T(8,128)(2,1)S(1)}) custom-call(s32[1]{0:T(128)} %bitcast.at, bf16[1024,3584]{1,0:T(8,128)(2,1)} %acts_hbm.3, bf16[1024,1024]{1,0:T(8,128)(2,1)} %grads_hbm.3, bf16[64,3584]{1,0:T(8,128)(2,1)} %bitcast.11, bf16[64,1024]{1,0:T(8,128)(2,1)} %bitcast.12), custom_call_target="tpu_custom_call" | custom-call | flops 603979776 | bytes 4718592 | tf_op jit(solution)/shard_map/pallas_call | solution.py:209
  3.6 0.5 %collective-permute-start = (f32[512,128]{1,0:T(8,128)S(1)}, f32[512,128]{1,0:T(8,128)S(1)}, u32[]{:S(2)}, u32[]{:S(2)}) collective-permute-start(f32[512,128]{1,0:T(8,128)S(1)} %get-tuple-element.14), channel_id=1, source_target_pairs={{0,1},{1,0},{2,3},{3,2},{4,5},{5,4},{6,7},{7,6},{8,9},{9,8},{10,11... | collective-permute-start | bytes 786440 | tf_op jit(solution)/shard_map/ppermute | solution.py:226
  4.2 0.0 copy-start
  4.2 0.0 copy-start.1
  4.2 2.4 %shard_map.66.kept = f32[512,128]{1,0:T(8,128)S(1)} custom-call(s32[1]{0:T(128)} %bitcast.at, bf16[1024,3584]{1,0:T(8,128)(2,1)} %acts_hbm.3, bf16[1024,1024]{1,0:T(8,128)(2,1)} %grads_hbm.3, bf16[128,4608]{1,0:T(8,128)(2,1)S(1)} %get-tuple-element.12.weights, bf16[3,512,512]{2,1,0:T(8,128)(2,1)S(1)} %get-tuple-element.13.early), custom_call_target="tpu_custom_call" | custom-call | flops 603979776 | bytes 4718592 | tf_op jit(solution)/shard_map/pallas_call | solution.py:227
  6.5 0.0 collective-permute-done.got
  6.5 0.2 shard_map.67
  6.7 2.7 %collective-permute-start.1 = (s16[144,128]{1,0:T(8,128)(2,1)S(1)}, s16[144,128]{1,0:T(8,128)(2,1)S(1)}, u32[]{:S(2)}, u32[]{:S(2)}) collective-permute-start(s16[144,128]{1,0:T(8,128)(2,1)S(1)} %get-tuple-element.16), channel_id=1, source_target_pairs={{0,2},{1,3},{2,0},{3,1},{4,6},{5,7},{6,4},{7,5},{8,10},{9,11},{10,... | collective-permute-start | bytes 110600 | tf_op jit(solution)/shard_map/ppermute | solution.py:249
  9.4 2.6 %collective-permute-start.2 = (s16[144,128]{1,0:T(8,128)(2,1)S(1)}, s16[144,128]{1,0:T(8,128)(2,1)S(1)}, u32[]{:S(2)}, u32[]{:S(2)}) collective-permute-start(s16[144,128]{1,0:T(8,128)(2,1)S(1)} %get-tuple-element.17), channel_id=1, source_target_pairs={{0,4},{1,5},{2,6},{3,7},{4,0},{5,1},{6,2},{7,3},{8,12},{9,13},{10,... | collective-permute-start | bytes 110600 | tf_op jit(solution)/shard_map/ppermute | solution.py:249
  12.0 0.0 collective-permute-start.3
  12.0 0.0 copy-done
  12.0 0.0 copy-done.1
  12.0 0.6 %shard_map.64.lives = f32[4,128]{1,0:T(4,128)S(1)} custom-call(s32[1,4]{1,0:T(1,128)S(1)} %copy-done, s32[1,4]{1,0:T(1,128)S(1)} %copy-done.1, s32[1]{0:T(128)} %bitcast.at), custom_call_target="tpu_custom_call" | custom-call | tf_op jit(solution)/shard_map/pallas_call | solution.py:252
  12.6 0.0 collective-permute-done.1.refs_0_
  12.6 2.5 %collective-permute-done.2.refs_1_ = s16[144,128]{1,0:T(8,128)(2,1)S(1)} collective-permute-done((s16[144,128]{1,0:T(8,128)(2,1)S(1)}, s16[144,128]{1,0:T(8,128)(2,1)S(1)}, u32[]{:S(2)}, u32[]{:S(2)}) %collective-permute-start.2) | collective-permute-done | bytes 36896 | tf_op jit(solution)/shard_map/ppermute | solution.py:249
  15.0 2.7 %collective-permute-done.3.refs_2_ = s16[144,128]{1,0:T(8,128)(2,1)S(1)} collective-permute-done((s16[144,128]{1,0:T(8,128)(2,1)S(1)}, s16[144,128]{1,0:T(8,128)(2,1)S(1)}, u32[]{:S(2)}, u32[]{:S(2)}) %collective-permute-start.3) | collective-permute-done | bytes 36896 | tf_op jit(solution)/shard_map/ppermute | solution.py:249
  17.7 0.2 shard_map.68
  18.0 10.0 %all_to_all.9 = f32[32,4,128]{2,1,0:T(4,128)S(1)} all-to-all(f32[32,4,128]{2,1,0:T(4,128)S(1)} %bitcast.10), channel_id=1, replica_groups=mesh['dp'=4,'tensor'=8] {'dp','tensor'}, dimensions={0} | all-to-all | bytes 131072 | tf_op jit(solution)/shard_map/all_to_all | solution.py:271
  28.0 0.6 %copy.9 = f32[1,4,4,128]{3,1,2,0:T(4,128)} copy(f32[1,4,4,128]{3,2,1,0:T(4,128)S(1)} %bitcast.13) | data formatting | bytes 16384
  (1 shorter events, 0.0 us)
Async XLA Ops:
  3.6 2.9 %collective-permute-start = (f32[512,128]{1,0:T(8,128)S(1)}, f32[512,128]{1,0:T(8,128)S(1)}, u32[]{:S(2)}, u32[]{:S(2)}) collective-permute-start(f32[512,128]{1,0:T(8,128)S(1)} %get-tuple-element.14), channel_id=1, source_target_pairs={{0,1},{1,0},{2,3},{3,2},{4,5},{5,4},{6,7},{7,6},{8,9},{9,8},{10,11... | collective-permute-start | bytes 786440 | tf_op jit(solution)/shard_map/ppermute | solution.py:226
  4.2 7.8 %copy-start = (s32[1,4]{1,0:T(1,128)S(1)}, s32[1,4]{1,0:T(1,128)}, u32[]{:S(2)}) copy-start(s32[1,4]{1,0:T(1,128)} %doc_len.1) | copy-start | bytes 52
  4.2 7.8 %copy-start.1 = (s32[1,4]{1,0:T(1,128)S(1)}, s32[1,4]{1,0:T(1,128)}, u32[]{:S(2)}) copy-start(s32[1,4]{1,0:T(1,128)} %doc_owner.1) | copy-start | bytes 52
  6.7 5.8 %collective-permute-start.1 = (s16[144,128]{1,0:T(8,128)(2,1)S(1)}, s16[144,128]{1,0:T(8,128)(2,1)S(1)}, u32[]{:S(2)}, u32[]{:S(2)}) collective-permute-start(s16[144,128]{1,0:T(8,128)(2,1)S(1)} %get-tuple-element.16), channel_id=1, source_target_pairs={{0,2},{1,3},{2,0},{3,1},{4,6},{5,7},{6,4},{7,5},{8,10},{9,11},{10,... | collective-permute-start | bytes 110600 | tf_op jit(solution)/shard_map/ppermute | solution.py:249
  9.4 5.6 %collective-permute-start.2 = (s16[144,128]{1,0:T(8,128)(2,1)S(1)}, s16[144,128]{1,0:T(8,128)(2,1)S(1)}, u32[]{:S(2)}, u32[]{:S(2)}) collective-permute-start(s16[144,128]{1,0:T(8,128)(2,1)S(1)} %get-tuple-element.17), channel_id=1, source_target_pairs={{0,4},{1,5},{2,6},{3,7},{4,0},{5,1},{6,2},{7,3},{8,12},{9,13},{10,... | collective-permute-start | bytes 110600 | tf_op jit(solution)/shard_map/ppermute | solution.py:249
  12.0 5.8 %collective-permute-start.3 = (s16[144,128]{1,0:T(8,128)(2,1)S(1)}, s16[144,128]{1,0:T(8,128)(2,1)S(1)}, u32[]{:S(2)}, u32[]{:S(2)}) collective-permute-start(s16[144,128]{1,0:T(8,128)(2,1)S(1)} %get-tuple-element.18), channel_id=1, source_target_pairs={{0,6},{1,7},{2,4},{3,5},{4,2},{5,3},{6,0},{7,1},{8,14},{9,15},{10,... | collective-permute-start | bytes 110600 | tf_op jit(solution)/shard_map/ppermute | solution.py:249

commit v5 on v3

--- a/solution.py
+++ b/solution.py
@@ -141,17 +141,6 @@
                 )
     grads = lax.dot_general(picked[...], other[...], NT, preferred_element_type=jnp.float32)
     out[...] = grads.reshape(out.shape)
-
-
-def collect(parts, out):
-    seqs, width = out.shape
-    lanes = parts.shape[1]
-    blocks = width // lanes
-    terms = parts.shape[0] // (seqs * blocks)
-    for s in range(seqs):
-        for c in range(blocks):
-            block = parts[pl.ds(s * terms * blocks + c, terms, stride=blocks), :]
-            out[pl.ds(s, 1), pl.ds(c * lanes, lanes)] = jnp.sum(block, axis=0, keepdims=True)
 
 
 def on_device(acts, out_grads, proj_in, proj_out, doc_lengths, owner_map):
@@ -222,13 +211,8 @@
     got = lax.all_to_all(
         grads.reshape(owners * rank // 2, lanes), ("dp", "tensor"), 0, 0, tiled=True
     )
-    return pl.pallas_call(
-        collect,
-        out_shape=jax.ShapeDtypeStruct((owners, rank * rank // split), jnp.float32),
-        in_specs=[vmem],
-        out_specs=vmem,
-        compiler_params=small,
-    )(got)
+    blocks = rank * rank // (split * lanes)
+    return jnp.sum(got.reshape(owners, split, blocks, lanes), 1).reshape(owners, blocks * lanes)
 
 
 def solution(mesh):

time: 29 us -> 29 us (level)
  Pallas kernels: 6.33 us -> 5.72 us
  local copies, waits for them, and re-layouts: 0.03 us -> 0.64 us
    pallas_call x1 -> x0, Pallas kernels: 0.61 us -> none  [on_device(): pl.pallas_call(collect, out_shape=jax.ShapeDtypeStruct((owners, rank * ra...]
    unnamed x4 -> x5, local copies, waits for them, and re-layouts: 0.01 us -> 0.61 us
where the time goes in v5:
time: 29 us; the launch traced here: 28.8 us
  blocking collectives  9.97 us (34%)
  waiting for transfers between devices  6.32 us (22%)
  starting transfers between devices  6.12 us (21%)
  Pallas kernels  5.72 us (20%)
  local copies, waits for them, and re-layouts  0.64 us (2%)
    all_to_all x1, blocking collectives, on_device(): lax.all_to_all(grads.reshape(owners * rank // 2, lanes), ('dp', 'tensor')...  9.97 us
    ppermute x3, starting transfers between devices, on_device(): lax.ppermute(block, 'tensor', [(i, i ^ 2 * m) for i in range(split)])  5.6 us
    ppermute x3, waiting for transfers between devices, on_device(): lax.ppermute(block, 'tensor', [(i, i ^ 2 * m) for i in range(split)])  5.16 us
    pallas_call x1, Pallas kernels, on_device(): pl.pallas_call(project, out_shape=pltpu.VMEM((length, lanes), jnp.float32...  4.72 us
    ppermute x1, waiting for transfers between devices, on_device(): got = lax.ppermute(sent, 'tensor', [(i, i ^ 1) for i in range(split)])  1.16 us
    unnamed x5, local copies, waits for them, and re-layouts  0.61 us
  transfers between devices with their start and end apart: 4, of which 3 were waited for; matrix products, arithmetic and copies ran while one was open for 0% of the time, Pallas kernels for 2%

profile of v5, /device:TPU:0, one launch (start us, length us, event | category | flops | bytes accessed | tf_op | source)
XLA Modules:
  0.0 28.8 jit_solution(5727035130777910782)
XLA Ops:
  0.0 0.0 copy-start
  0.0 0.0 copy-start.1
  0.0 4.7 %shard_map.65.sums = f32[1024,128]{1,0:T(8,128)S(1)} custom-call(bf16[1024,3584]{1,0:T(8,128)(2,1)} %acts_hbm.1, bf16[1024,1024]{1,0:T(8,128)(2,1)} %grads_hbm.1, bf16[64,3584]{1,0:T(8,128)(2,1)} %bitcast.11, bf16[64,1024]{1,0:T(8,128)(2,1)} %bitcast.12), custom_call_target="tpu_custom_call" | custom-call | tf_op jit(solution)/shard_map/pallas_call | solution.py:164
  4.8 0.5 %collective-permute-start = (f32[512,128]{1,0:T(8,128)S(1)}, f32[512,128]{1,0:T(8,128)S(1)}, u32[]{:S(2)}, u32[]{:S(2)}) collective-permute-start(f32[512,128]{1,0:T(8,128)S(1)} %constant_dynamic-slice_fusion), channel_id=1, source_target_pairs={{0,1},{1,0},{2,3},{3,2},{4,5},{5,4},{6,7},{7,6},{8,9},{9,8},{10,11... | collective-permute-start | bytes 786440 | tf_op jit(solution)/shard_map/ppermute | solution.py:178
  5.3 1.2 %collective-permute-done.got = f32[512,128]{1,0:T(8,128)S(1)} collective-permute-done((f32[512,128]{1,0:T(8,128)S(1)}, f32[512,128]{1,0:T(8,128)S(1)}, u32[]{:S(2)}, u32[]{:S(2)}) %collective-permute-start) | collective-permute-done | bytes 262176 | tf_op jit(solution)/shard_map/ppermute | solution.py:178
  6.5 0.2 shard_map.66
  6.6 3.0 %collective-permute-start.1 = (s16[144,128]{1,0:T(8,128)(2,1)S(1)}, s16[144,128]{1,0:T(8,128)(2,1)S(1)}, u32[]{:S(2)}, u32[]{:S(2)}) collective-permute-start(s16[144,128]{1,0:T(8,128)(2,1)S(1)} %get-tuple-element.10), channel_id=1, source_target_pairs={{0,2},{1,3},{2,0},{3,1},{4,6},{5,7},{6,4},{7,5},{8,10},{9,11},{10,... | collective-permute-start | bytes 110600 | tf_op jit(solution)/shard_map/ppermute | solution.py:189
  9.6 2.6 %collective-permute-start.2 = (s16[144,128]{1,0:T(8,128)(2,1)S(1)}, s16[144,128]{1,0:T(8,128)(2,1)S(1)}, u32[]{:S(2)}, u32[]{:S(2)}) collective-permute-start(s16[144,128]{1,0:T(8,128)(2,1)S(1)} %get-tuple-element.11), channel_id=1, source_target_pairs={{0,4},{1,5},{2,6},{3,7},{4,0},{5,1},{6,2},{7,3},{8,12},{9,13},{10,... | collective-permute-start | bytes 110600 | tf_op jit(solution)/shard_map/ppermute | solution.py:189
  12.2 0.0 collective-permute-start.3
  12.2 0.0 copy-done
  12.2 0.0 copy-done.1
  12.2 0.6 %shard_map.64.lives = f32[4,128]{1,0:T(4,128)S(1)} custom-call(s32[1,4]{1,0:T(1,128)S(1)} %copy-done, s32[1,4]{1,0:T(1,128)S(1)} %copy-done.1, s32[1]{0:T(128)} %bitcast.at), custom_call_target="tpu_custom_call" | custom-call | tf_op jit(solution)/shard_map/pallas_call | solution.py:192
  12.8 0.0 collective-permute-done.1.refs_0_
  12.8 2.4 %collective-permute-done.2.refs_1_ = s16[144,128]{1,0:T(8,128)(2,1)S(1)} collective-permute-done((s16[144,128]{1,0:T(8,128)(2,1)S(1)}, s16[144,128]{1,0:T(8,128)(2,1)S(1)}, u32[]{:S(2)}, u32[]{:S(2)}) %collective-permute-start.2) | collective-permute-done | bytes 36896 | tf_op jit(solution)/shard_map/ppermute | solution.py:189
  15.2 2.8 %collective-permute-done.3.refs_2_ = s16[144,128]{1,0:T(8,128)(2,1)S(1)} collective-permute-done((s16[144,128]{1,0:T(8,128)(2,1)S(1)}, s16[144,128]{1,0:T(8,128)(2,1)S(1)}, u32[]{:S(2)}, u32[]{:S(2)}) %collective-permute-start.3) | collective-permute-done | bytes 36896 | tf_op jit(solution)/shard_map/ppermute | solution.py:189
  18.0 0.2 shard_map.67
  18.2 10.0 %all_to_all.9 = f32[32,4,128]{2,1,0:T(4,128)S(1)} all-to-all(f32[32,4,128]{2,1,0:T(4,128)S(1)} %bitcast.10), channel_id=1, replica_groups=mesh['dp'=4,'tensor'=8] {'dp','tensor'}, dimensions={0} | all-to-all | bytes 131072 | tf_op jit(solution)/shard_map/all_to_all | solution.py:211
  28.2 0.6 %copy.9 = f32[1,4,4,128]{3,1,2,0:T(4,128)} copy(f32[1,4,4,128]{3,2,1,0:T(4,128)S(1)} %bitcast.13) | data formatting | bytes 16384
  (2 shorter events, 0.0 us)
Async XLA Ops:
  0.0 12.2 %copy-start = (s32[1,4]{1,0:T(1,128)S(1)}, s32[1,4]{1,0:T(1,128)}, u32[]{:S(2)}) copy-start(s32[1,4]{1,0:T(1,128)} %doc_len.1) | copy-start | bytes 52
  0.0 12.2 %copy-start.1 = (s32[1,4]{1,0:T(1,128)S(1)}, s32[1,4]{1,0:T(1,128)}, u32[]{:S(2)}) copy-start(s32[1,4]{1,0:T(1,128)} %doc_owner.1) | copy-start | bytes 52
  4.8 1.7 %collective-permute-start = (f32[512,128]{1,0:T(8,128)S(1)}, f32[512,128]{1,0:T(8,128)S(1)}, u32[]{:S(2)}, u32[]{:S(2)}) collective-permute-start(f32[512,128]{1,0:T(8,128)S(1)} %constant_dynamic-slice_fusion), channel_id=1, source_target_pairs={{0,1},{1,0},{2,3},{3,2},{4,5},{5,4},{6,7},{7,6},{8,9},{9,8},{10,11... | collective-permute-start | bytes 786440 | tf_op jit(solution)/shard_map/ppermute | solution.py:178
  6.6 6.2 %collective-permute-start.1 = (s16[144,128]{1,0:T(8,128)(2,1)S(1)}, s16[144,128]{1,0:T(8,128)(2,1)S(1)}, u32[]{:S(2)}, u32[]{:S(2)}) collective-permute-start(s16[144,128]{1,0:T(8,128)(2,1)S(1)} %get-tuple-element.10), channel_id=1, source_target_pairs={{0,2},{1,3},{2,0},{3,1},{4,6},{5,7},{6,4},{7,5},{8,10},{9,11},{10,... | collective-permute-start | bytes 110600 | tf_op jit(solution)/shard_map/ppermute | solution.py:189
  9.6 5.6 %collective-permute-start.2 = (s16[144,128]{1,0:T(8,128)(2,1)S(1)}, s16[144,128]{1,0:T(8,128)(2,1)S(1)}, u32[]{:S(2)}, u32[]{:S(2)}) collective-permute-start(s16[144,128]{1,0:T(8,128)(2,1)S(1)} %get-tuple-element.11), channel_id=1, source_target_pairs={{0,4},{1,5},{2,6},{3,7},{4,0},{5,1},{6,2},{7,3},{8,12},{9,13},{10,... | collective-permute-start | bytes 110600 | tf_op jit(solution)/shard_map/ppermute | solution.py:189
  12.2 5.8 %collective-permute-start.3 = (s16[144,128]{1,0:T(8,128)(2,1)S(1)}, s16[144,128]{1,0:T(8,128)(2,1)S(1)}, u32[]{:S(2)}, u32[]{:S(2)}) collective-permute-start(s16[144,128]{1,0:T(8,128)(2,1)S(1)} %get-tuple-element.12), channel_id=1, source_target_pairs={{0,6},{1,7},{2,4},{3,5},{4,2},{5,3},{6,0},{7,1},{8,14},{9,15},{10,... | collective-permute-start | bytes 110600 | tf_op jit(solution)/shard_map/ppermute | solution.py:189

commit v6 on v4

--- a/solution.py
+++ b/solution.py
@@ -236,7 +236,7 @@
         compiler_params=medium,
         cost_estimate=cost,
     )(at, acts, out_grads, weights, early)
-    order = tuple(range(1, pairs))
+    order = tuple(range(pairs - 1, 0, -1))
     own, *coded = pl.pallas_call(
         functools.partial(code, order),
         out_shape=(pltpu.VMEM((lanes, tokens), jnp.float32),)

time: 28.8 us -> 28.8 us (level)
  waiting for transfers between devices: 5.16 us -> 3.63 us
  blocking collectives: 10 us -> 11.5 us
    ppermute x3, waiting for transfers between devices: 5.16 us -> 3.63 us  [on_device(): lax.ppermute(block, 'tensor', [(i, i ^ 2 * m) for i in range(split)])]
    all_to_all x1, blocking collectives: 10 us -> 11.5 us  [on_device(): lax.all_to_all(grads.reshape(owners * rank // 2, lanes), ('dp', 'tensor')...]
where the time goes in v6:
time: 28.8 us; the launch traced here: 28.6 us
  blocking collectives  11.5 us (40%)
  Pallas kernels  6.98 us (24%)
  starting transfers between devices  5.85 us (20%)
  waiting for transfers between devices  3.63 us (13%)
  local copies, waits for them, and re-layouts  0.61 us (2%)
    all_to_all x1, blocking collectives, on_device(): lax.all_to_all(grads.reshape(owners * rank // 2, lanes), ('dp', 'tensor')...  11.5 us
    ppermute x3, starting transfers between devices, on_device(): lax.ppermute(block, 'tensor', [(i, i ^ 2 * m) for i in range(split)])  5.32 us
    ppermute x3, waiting for transfers between devices, on_device(): lax.ppermute(block, 'tensor', [(i, i ^ 2 * m) for i in range(split)])  3.63 us
    pallas_call x1, Pallas kernels, on_device(): pl.pallas_call(project_sent, out_shape=(sums, pltpu.VMEM((lanes, hidden +...  3.61 us
    pallas_call x1, Pallas kernels, on_device(): pl.pallas_call(project_kept, out_shape=sums, in_specs=[smem, hbm, hbm, vm...  2.36 us
    unnamed x5, local copies, waits for them, and re-layouts  0.61 us
  transfers between devices with their start and end apart: 4, of which 2 were waited for; matrix products, arithmetic and copies ran while one was open for 0% of the time, Pallas kernels for 10%

profile of v6, /device:TPU:0, one launch (start us, length us, event | category | flops | bytes accessed | tf_op | source)
XLA Modules:
  0.0 28.6 jit_solution(10420491702796141993)
XLA Ops:
  0.0 3.6 %shard_map.65 = (f32[512,128]{1,0:T(8,128)S(1)}, bf16[128,4608]{1,0:T(8,128)(2,1)S(1)}, bf16[3,512,512]{2,1,0:T(8,128)(2,1)S(1)}) custom-call(s32[1]{0:T(128)} %bitcast.at, bf16[1024,3584]{1,0:T(8,128)(2,1)} %acts_hbm.3, bf16[1024,1024]{1,0:T(8,128)(2,1)} %grads_hbm.3, bf16[64,3584]{1,0:T(8,128)(2,1)} %bitcast.11, bf16[64,1024]{1,0:T(8,128)(2,1)} %bitcast.12), custom_call_target="tpu_custom_call" | custom-call | flops 603979776 | bytes 4718592 | tf_op jit(solution)/shard_map/pallas_call | solution.py:209
  3.6 0.5 %collective-permute-start = (f32[512,128]{1,0:T(8,128)S(1)}, f32[512,128]{1,0:T(8,128)S(1)}, u32[]{:S(2)}, u32[]{:S(2)}) collective-permute-start(f32[512,128]{1,0:T(8,128)S(1)} %get-tuple-element.14), channel_id=1, source_target_pairs={{0,1},{1,0},{2,3},{3,2},{4,5},{5,4},{6,7},{7,6},{8,9},{9,8},{10,11... | collective-permute-start | bytes 786440 | tf_op jit(solution)/shard_map/ppermute | solution.py:226
  4.2 0.0 copy-start
  4.2 0.0 copy-start.1
  4.2 2.4 %shard_map.66.kept = f32[512,128]{1,0:T(8,128)S(1)} custom-call(s32[1]{0:T(128)} %bitcast.at, bf16[1024,3584]{1,0:T(8,128)(2,1)} %acts_hbm.3, bf16[1024,1024]{1,0:T(8,128)(2,1)} %grads_hbm.3, bf16[128,4608]{1,0:T(8,128)(2,1)S(1)} %get-tuple-element.12.weights, bf16[3,512,512]{2,1,0:T(8,128)(2,1)S(1)} %get-tuple-element.13.early), custom_call_target="tpu_custom_call" | custom-call | flops 603979776 | bytes 4718592 | tf_op jit(solution)/shard_map/pallas_call | solution.py:227
  6.5 0.0 collective-permute-done.got
  6.5 0.2 shard_map.67
  6.7 4.7 %collective-permute-start.1 = (s16[144,128]{1,0:T(8,128)(2,1)S(1)}, s16[144,128]{1,0:T(8,128)(2,1)S(1)}, u32[]{:S(2)}, u32[]{:S(2)}) collective-permute-start(s16[144,128]{1,0:T(8,128)(2,1)S(1)} %get-tuple-element.16), channel_id=1, source_target_pairs={{0,6},{1,7},{2,4},{3,5},{4,2},{5,3},{6,0},{7,1},{8,14},{9,15},{10,... | collective-permute-start | bytes 110600 | tf_op jit(solution)/shard_map/ppermute | solution.py:249
  11.4 0.0 collective-permute-start.2
  11.4 0.6 %collective-permute-start.3 = (s16[144,128]{1,0:T(8,128)(2,1)S(1)}, s16[144,128]{1,0:T(8,128)(2,1)S(1)}, u32[]{:S(2)}, u32[]{:S(2)}) collective-permute-start(s16[144,128]{1,0:T(8,128)(2,1)S(1)} %get-tuple-element.18), channel_id=1, source_target_pairs={{0,2},{1,3},{2,0},{3,1},{4,6},{5,7},{6,4},{7,5},{8,10},{9,11},{10,... | collective-permute-start | bytes 110600 | tf_op jit(solution)/shard_map/ppermute | solution.py:249
  12.1 0.0 copy-done
  12.1 0.0 copy-done.1
  12.1 0.6 %shard_map.64.lives = f32[4,128]{1,0:T(4,128)S(1)} custom-call(s32[1,4]{1,0:T(1,128)S(1)} %copy-done, s32[1,4]{1,0:T(1,128)S(1)} %copy-done.1, s32[1]{0:T(128)} %bitcast.at), custom_call_target="tpu_custom_call" | custom-call | tf_op jit(solution)/shard_map/pallas_call | solution.py:252
  12.6 1.0 %collective-permute-done.1.refs_0_ = s16[144,128]{1,0:T(8,128)(2,1)S(1)} collective-permute-done((s16[144,128]{1,0:T(8,128)(2,1)S(1)}, s16[144,128]{1,0:T(8,128)(2,1)S(1)}, u32[]{:S(2)}, u32[]{:S(2)}) %collective-permute-start.1) | collective-permute-done | bytes 36896 | tf_op jit(solution)/shard_map/ppermute | solution.py:249
  13.6 2.7 %collective-permute-done.2.refs_1_ = s16[144,128]{1,0:T(8,128)(2,1)S(1)} collective-permute-done((s16[144,128]{1,0:T(8,128)(2,1)S(1)}, s16[144,128]{1,0:T(8,128)(2,1)S(1)}, u32[]{:S(2)}, u32[]{:S(2)}) %collective-permute-start.2) | collective-permute-done | bytes 36896 | tf_op jit(solution)/shard_map/ppermute | solution.py:249
  16.3 0.0 collective-permute-done.3.refs_2_
  16.3 0.2 shard_map.68
  16.5 11.5 %all_to_all.9 = f32[32,4,128]{2,1,0:T(4,128)S(1)} all-to-all(f32[32,4,128]{2,1,0:T(4,128)S(1)} %bitcast.10), channel_id=1, replica_groups=mesh['dp'=4,'tensor'=8] {'dp','tensor'}, dimensions={0} | all-to-all | bytes 131072 | tf_op jit(solution)/shard_map/all_to_all | solution.py:271
  28.0 0.6 %copy.9 = f32[1,4,4,128]{3,1,2,0:T(4,128)} copy(f32[1,4,4,128]{3,2,1,0:T(4,128)S(1)} %bitcast.13) | data formatting | bytes 16384
  (1 shorter events, 0.0 us)
Async XLA Ops:
  3.6 2.9 %collective-permute-start = (f32[512,128]{1,0:T(8,128)S(1)}, f32[512,128]{1,0:T(8,128)S(1)}, u32[]{:S(2)}, u32[]{:S(2)}) collective-permute-start(f32[512,128]{1,0:T(8,128)S(1)} %get-tuple-element.14), channel_id=1, source_target_pairs={{0,1},{1,0},{2,3},{3,2},{4,5},{5,4},{6,7},{7,6},{8,9},{9,8},{10,11... | collective-permute-start | bytes 786440 | tf_op jit(solution)/shard_map/ppermute | solution.py:226
  4.2 7.9 %copy-start = (s32[1,4]{1,0:T(1,128)S(1)}, s32[1,4]{1,0:T(1,128)}, u32[]{:S(2)}) copy-start(s32[1,4]{1,0:T(1,128)} %doc_len.1) | copy-start | bytes 52
  4.2 7.9 %copy-start.1 = (s32[1,4]{1,0:T(1,128)S(1)}, s32[1,4]{1,0:T(1,128)}, u32[]{:S(2)}) copy-start(s32[1,4]{1,0:T(1,128)} %doc_owner.1) | copy-start | bytes 52
  6.7 6.9 %collective-permute-start.1 = (s16[144,128]{1,0:T(8,128)(2,1)S(1)}, s16[144,128]{1,0:T(8,128)(2,1)S(1)}, u32[]{:S(2)}, u32[]{:S(2)}) collective-permute-start(s16[144,128]{1,0:T(8,128)(2,1)S(1)} %get-tuple-element.16), channel_id=1, source_target_pairs={{0,6},{1,7},{2,4},{3,5},{4,2},{5,3},{6,0},{7,1},{8,14},{9,15},{10,... | collective-permute-start | bytes 110600 | tf_op jit(solution)/shard_map/ppermute | solution.py:249
  11.4 4.9 %collective-permute-start.2 = (s16[144,128]{1,0:T(8,128)(2,1)S(1)}, s16[144,128]{1,0:T(8,128)(2,1)S(1)}, u32[]{:S(2)}, u32[]{:S(2)}) collective-permute-start(s16[144,128]{1,0:T(8,128)(2,1)S(1)} %get-tuple-element.17), channel_id=1, source_target_pairs={{0,4},{1,5},{2,6},{3,7},{4,0},{5,1},{6,2},{7,3},{8,12},{9,13},{10,... | collective-permute-start | bytes 110600 | tf_op jit(solution)/shard_map/ppermute | solution.py:249
  11.4 4.9 %collective-permute-start.3 = (s16[144,128]{1,0:T(8,128)(2,1)S(1)}, s16[144,128]{1,0:T(8,128)(2,1)S(1)}, u32[]{:S(2)}, u32[]{:S(2)}) collective-permute-start(s16[144,128]{1,0:T(8,128)(2,1)S(1)} %get-tuple-element.18), channel_id=1, source_target_pairs={{0,2},{1,3},{2,0},{3,1},{4,6},{5,7},{6,4},{7,5},{8,10},{9,11},{10,... | collective-permute-start | bytes 110600 | tf_op jit(solution)/shard_map/ppermute | solution.py:249

commit v7 on v6

--- a/solution.py
+++ b/solution.py
@@ -55,7 +55,7 @@
     loads[0].start()
     copies[0].start()
     loads[1].start()
-    for copy in copies[1:8]:
+    for copy in copies[1:6]:
         copy.start()
     weights[pl.ds(0, rank), pl.ds(0, width)] = jnp.zeros((rank, width), weights.dtype)
     weights[pl.ds(rank, rank), pl.ds(width, hidden)] = jnp.zeros((rank, hidden), weights.dtype)
@@ -64,8 +64,8 @@
         if i * depth == width:
             loads[1].wait()
         copies[i].wait()
-        if i + 8 < len(copies):
-            copies[i + 8].start()
+        if i + 6 < len(copies):
+            copies[i + 6].start()
         add_product(sent, i == 0, held.at[i], weights[:, i * depth : (i + 1) * depth])
     for copy in copies[chunks:]:
         copy.wait()
@@ -79,7 +79,7 @@
         columns_of(acts_hbm, grads_hbm, core * half, half, depth, ready + i, held.at[i], sems.at[i])
         for i in range(rest)
     ]
-    for copy in copies[:8]:
+    for copy in copies[:6]:
         copy.start()
     for i in range(ready + rest):
         if i < ready:
@@ -87,8 +87,8 @@
         else:
             left = held.at[i - ready]
             copies[i - ready].wait()
-            if i - ready + 8 < rest:
-                copies[i - ready + 8].start()
+            if i - ready + 6 < rest:
+                copies[i - ready + 6].start()
         add_product(kept, i == 0, left, weights[:, i * depth : (i + 1) * depth])
 
 

time: 28.8 us -> 28.8 us (level)
  no operation moved by 1% of the time
where the time goes in v7:
time: 28.8 us; the launch traced here: 28.6 us
  blocking collectives  11.5 us (40%)
  Pallas kernels  7.02 us (24%)
  starting transfers between devices  5.85 us (20%)
  waiting for transfers between devices  3.63 us (13%)
  local copies, waits for them, and re-layouts  0.61 us (2%)
    all_to_all x1, blocking collectives, on_device(): lax.all_to_all(grads.reshape(owners * rank // 2, lanes), ('dp', 'tensor')...  11.5 us
    ppermute x3, starting transfers between devices, on_device(): lax.ppermute(block, 'tensor', [(i, i ^ 2 * m) for i in range(split)])  5.34 us
    pallas_call x1, Pallas kernels, on_device(): pl.pallas_call(project_sent, out_shape=(sums, pltpu.VMEM((lanes, hidden +...  3.66 us
    ppermute x3, waiting for transfers between devices, on_device(): lax.ppermute(block, 'tensor', [(i, i ^ 2 * m) for i in range(split)])  3.63 us
    pallas_call x1, Pallas kernels, on_device(): pl.pallas_call(project_kept, out_shape=sums, in_specs=[smem, hbm, hbm, vm...  2.35 us
    unnamed x5, local copies, waits for them, and re-layouts  0.61 us
  transfers between devices with their start and end apart: 4, of which 2 were waited for; matrix products, arithmetic and copies ran while one was open for 0% of the time, Pallas kernels for 10%

profile of v7, /device:TPU:0, one launch (start us, length us, event | category | flops | bytes accessed | tf_op | source)
XLA Modules:
  0.0 28.6 jit_solution(13750076192091308617)
XLA Ops:
  0.0 3.7 %shard_map.65 = (f32[512,128]{1,0:T(8,128)S(1)}, bf16[128,4608]{1,0:T(8,128)(2,1)S(1)}, bf16[3,512,512]{2,1,0:T(8,128)(2,1)S(1)}) custom-call(s32[1]{0:T(128)} %bitcast.at, bf16[1024,3584]{1,0:T(8,128)(2,1)} %acts_hbm.3, bf16[1024,1024]{1,0:T(8,128)(2,1)} %grads_hbm.3, bf16[64,3584]{1,0:T(8,128)(2,1)} %bitcast.11, bf16[64,1024]{1,0:T(8,128)(2,1)} %bitcast.12), custom_call_target="tpu_custom_call" | custom-call | flops 603979776 | bytes 4718592 | tf_op jit(solution)/shard_map/pallas_call | solution.py:209
  3.7 0.5 %collective-permute-start = (f32[512,128]{1,0:T(8,128)S(1)}, f32[512,128]{1,0:T(8,128)S(1)}, u32[]{:S(2)}, u32[]{:S(2)}) collective-permute-start(f32[512,128]{1,0:T(8,128)S(1)} %get-tuple-element.14), channel_id=1, source_target_pairs={{0,1},{1,0},{2,3},{3,2},{4,5},{5,4},{6,7},{7,6},{8,9},{9,8},{10,11... | collective-permute-start | bytes 786440 | tf_op jit(solution)/shard_map/ppermute | solution.py:226
  4.2 0.0 copy-start
  4.2 0.0 copy-start.1
  4.2 2.4 %shard_map.66.kept = f32[512,128]{1,0:T(8,128)S(1)} custom-call(s32[1]{0:T(128)} %bitcast.at, bf16[1024,3584]{1,0:T(8,128)(2,1)} %acts_hbm.3, bf16[1024,1024]{1,0:T(8,128)(2,1)} %grads_hbm.3, bf16[128,4608]{1,0:T(8,128)(2,1)S(1)} %get-tuple-element.12.weights, bf16[3,512,512]{2,1,0:T(8,128)(2,1)S(1)} %get-tuple-element.13.early), custom_call_target="tpu_custom_call" | custom-call | flops 603979776 | bytes 4718592 | tf_op jit(solution)/shard_map/pallas_call | solution.py:227
  6.6 0.0 collective-permute-done.got
  6.6 0.2 shard_map.67
  6.8 4.7 %collective-permute-start.1 = (s16[144,128]{1,0:T(8,128)(2,1)S(1)}, s16[144,128]{1,0:T(8,128)(2,1)S(1)}, u32[]{:S(2)}, u32[]{:S(2)}) collective-permute-start(s16[144,128]{1,0:T(8,128)(2,1)S(1)} %get-tuple-element.16), channel_id=1, source_target_pairs={{0,6},{1,7},{2,4},{3,5},{4,2},{5,3},{6,0},{7,1},{8,14},{9,15},{10,... | collective-permute-start | bytes 110600 | tf_op jit(solution)/shard_map/ppermute | solution.py:249
  11.4 0.0 collective-permute-start.2
  11.4 0.6 %collective-permute-start.3 = (s16[144,128]{1,0:T(8,128)(2,1)S(1)}, s16[144,128]{1,0:T(8,128)(2,1)S(1)}, u32[]{:S(2)}, u32[]{:S(2)}) collective-permute-start(s16[144,128]{1,0:T(8,128)(2,1)S(1)} %get-tuple-element.18), channel_id=1, source_target_pairs={{0,2},{1,3},{2,0},{3,1},{4,6},{5,7},{6,4},{7,5},{8,10},{9,11},{10,... | collective-permute-start | bytes 110600 | tf_op jit(solution)/shard_map/ppermute | solution.py:249
  12.1 0.0 copy-done
  12.1 0.0 copy-done.1
  12.1 0.6 %shard_map.64.lives = f32[4,128]{1,0:T(4,128)S(1)} custom-call(s32[1,4]{1,0:T(1,128)S(1)} %copy-done, s32[1,4]{1,0:T(1,128)S(1)} %copy-done.1, s32[1]{0:T(128)} %bitcast.at), custom_call_target="tpu_custom_call" | custom-call | tf_op jit(solution)/shard_map/pallas_call | solution.py:252
  12.7 0.9 %collective-permute-done.1.refs_0_ = s16[144,128]{1,0:T(8,128)(2,1)S(1)} collective-permute-done((s16[144,128]{1,0:T(8,128)(2,1)S(1)}, s16[144,128]{1,0:T(8,128)(2,1)S(1)}, u32[]{:S(2)}, u32[]{:S(2)}) %collective-permute-start.1) | collective-permute-done | bytes 36896 | tf_op jit(solution)/shard_map/ppermute | solution.py:249
  13.6 2.7 %collective-permute-done.2.refs_1_ = s16[144,128]{1,0:T(8,128)(2,1)S(1)} collective-permute-done((s16[144,128]{1,0:T(8,128)(2,1)S(1)}, s16[144,128]{1,0:T(8,128)(2,1)S(1)}, u32[]{:S(2)}, u32[]{:S(2)}) %collective-permute-start.2) | collective-permute-done | bytes 36896 | tf_op jit(solution)/shard_map/ppermute | solution.py:249
  16.3 0.0 collective-permute-done.3.refs_2_
  16.3 0.2 shard_map.68
  16.6 11.5 %all_to_all.9 = f32[32,4,128]{2,1,0:T(4,128)S(1)} all-to-all(f32[32,4,128]{2,1,0:T(4,128)S(1)} %bitcast.10), channel_id=1, replica_groups=mesh['dp'=4,'tensor'=8] {'dp','tensor'}, dimensions={0} | all-to-all | bytes 131072 | tf_op jit(solution)/shard_map/all_to_all | solution.py:271
  28.0 0.6 %copy.9 = f32[1,4,4,128]{3,1,2,0:T(4,128)} copy(f32[1,4,4,128]{3,2,1,0:T(4,128)S(1)} %bitcast.13) | data formatting | bytes 16384
  (1 shorter events, 0.0 us)
Async XLA Ops:
  3.7 2.9 %collective-permute-start = (f32[512,128]{1,0:T(8,128)S(1)}, f32[512,128]{1,0:T(8,128)S(1)}, u32[]{:S(2)}, u32[]{:S(2)}) collective-permute-start(f32[512,128]{1,0:T(8,128)S(1)} %get-tuple-element.14), channel_id=1, source_target_pairs={{0,1},{1,0},{2,3},{3,2},{4,5},{5,4},{6,7},{7,6},{8,9},{9,8},{10,11... | collective-permute-start | bytes 786440 | tf_op jit(solution)/shard_map/ppermute | solution.py:226
  4.2 7.9 %copy-start = (s32[1,4]{1,0:T(1,128)S(1)}, s32[1,4]{1,0:T(1,128)}, u32[]{:S(2)}) copy-start(s32[1,4]{1,0:T(1,128)} %doc_len.1) | copy-start | bytes 52
  4.2 7.9 %copy-start.1 = (s32[1,4]{1,0:T(1,128)S(1)}, s32[1,4]{1,0:T(1,128)}, u32[]{:S(2)}) copy-start(s32[1,4]{1,0:T(1,128)} %doc_owner.1) | copy-start | bytes 52
  6.8 6.9 %collective-permute-start.1 = (s16[144,128]{1,0:T(8,128)(2,1)S(1)}, s16[144,128]{1,0:T(8,128)(2,1)S(1)}, u32[]{:S(2)}, u32[]{:S(2)}) collective-permute-start(s16[144,128]{1,0:T(8,128)(2,1)S(1)} %get-tuple-element.16), channel_id=1, source_target_pairs={{0,6},{1,7},{2,4},{3,5},{4,2},{5,3},{6,0},{7,1},{8,14},{9,15},{10,... | collective-permute-start | bytes 110600 | tf_op jit(solution)/shard_map/ppermute | solution.py:249
  11.4 4.9 %collective-permute-start.2 = (s16[144,128]{1,0:T(8,128)(2,1)S(1)}, s16[144,128]{1,0:T(8,128)(2,1)S(1)}, u32[]{:S(2)}, u32[]{:S(2)}) collective-permute-start(s16[144,128]{1,0:T(8,128)(2,1)S(1)} %get-tuple-element.17), channel_id=1, source_target_pairs={{0,4},{1,5},{2,6},{3,7},{4,0},{5,1},{6,2},{7,3},{8,12},{9,13},{10,... | collective-permute-start | bytes 110600 | tf_op jit(solution)/shard_map/ppermute | solution.py:249
  11.4 4.9 %collective-permute-start.3 = (s16[144,128]{1,0:T(8,128)(2,1)S(1)}, s16[144,128]{1,0:T(8,128)(2,1)S(1)}, u32[]{:S(2)}, u32[]{:S(2)}) collective-permute-start(s16[144,128]{1,0:T(8,128)(2,1)S(1)} %get-tuple-element.18), channel_id=1, source_target_pairs={{0,2},{1,3},{2,0},{3,1},{4,6},{5,7},{6,4},{7,5},{8,10},{9,11},{10,... | collective-permute-start | bytes 110600 | tf_op jit(solution)/shard_map/ppermute | solution.py:249
